TPU v7x, 32 devices: a whole 2x2x4 slice. The times are simulated.
32 devices in a mesh: dp: 16 (over z, y, core), narrow: 2 (over x).
Axes of the slice: x: 2, y: 2, z: 4, core: 2. Of those that a mesh axis runs over, the one named last changes fastest.
Arguments:
- tokens: bfloat16 [60928, 384], P(('dp', 'narrow')), may hold values from -6 to 6
- attn_weights: bfloat16 [1536, 192], P(('dp', 'narrow')), may hold values from -4 to 4
- norm_params: float32 [3, 2, 192], replicated, may hold values from -1 to 2
- w_in: bfloat16 [2, 192, 2, 256], P(None, None, None, 'narrow'), may hold values from -0.4375 to 0.4375
- w_out: bfloat16 [2, 256, 192], P(None, 'narrow'), may hold values from -0.375 to 0.375
- cotangent: bfloat16 [60928, 384], P(('dp', 'narrow')), may hold values from -6 to 6
Outputs:
- result: bfloat16 [60928, 384], P(('dp', 'narrow'))
- input_grad: float32 [60928, 384], P(('dp', 'narrow'))
- attn_grad: float32 [1536, 192], P(('dp', 'narrow'))
- norm_grad: float32 [3, 2, 192], replicated
- w_in_grad: float32 [2, 192, 2, 256], P(None, None, None, 'narrow')
- w_out_grad: float32 [2, 256, 192], P(None, 'narrow')
All inputs are finite; a program needn't handle non-finite values.
Results may differ from a plain program's by a relative error of at most 0.024.
Values may be sent and summed in bfloat16 or wider, within the bound.
No kernel may reach another device: no remote copies, remote signals or barrier semaphores. Data moves between devices by JAX's collectives and lax.ppermute only.
A program may use at most 256 MiB of HBM per device.

v0:
```python
import math

import jax
import jax.numpy as jnp
from jax import lax
from jax.experimental import pallas as pl
from jax.experimental.pallas import tpu as pltpu
from jax.sharding import PartitionSpec as P

HEADS = 8
HEAD = 24
SLOT = 32
WIDE = HEADS * SLOT
D = HEADS * HEAD
FF = 256
FFH = FF // 2
LAYERS = 2
NORMS = 2 * LAYERS - 1
SEQ = 476
PAIRS = SEQ // 2
KEYS = 240
HALF = 256
LANES = 2 * HALF
EPS = 1e-05
SCALE = HEAD ** (-0.5)
LOG2E = math.log2(math.e)
ATTN_ROWS = LAYERS * 4 * D

GROUP = 8
NEAR = (0, 1, 4, 5)
TWIN = 2
WIN_PART = LAYERS * D // 4
WOUT_PART = LAYERS * FFH // 4
ATTN_PART = ATTN_ROWS // GROUP
OFF_WOUT = ATTN_PART
OFF_NORM = OFF_WOUT + WOUT_PART
OFF_WIN = OFF_NORM + 16
PAY_ROWS = OFF_WIN + WIN_PART

bf16 = jnp.bfloat16
f32 = jnp.float32
AXES = ("dp", "narrow")

VMEM_BYTES = 60 * 1024 * 1024


def mm(left, right):
    return jnp.dot(left, right, preferred_element_type=f32)


def mm_nt(left, right):
    return lax.dot_general(left, right, (((1,), (1,)), ((), ())), preferred_element_type=f32)


def sigmoid(value):
    return 0.5 + 0.5 * jnp.tanh(0.5 * value)


def fold_lanes(value):
    return value[:, 0:128] + value[:, 128:256] + value[:, 256:384] + value[:, 384:512]


def norm_forward(stream, gain, shift):
    center = stream - jnp.sum(stream, axis=0, keepdims=True) * (1.0 / D)
    inverse = lax.rsqrt(jnp.sum(center * center, axis=0, keepdims=True) * (1.0 / D) + EPS)
    unit = center * inverse
    return (unit * gain + shift, unit, inverse)


def norm_backward(grad, unit, inverse, gain):
    scaled = grad * gain
    mean = jnp.sum(scaled, axis=0, keepdims=True) * (1.0 / D)
    slope = jnp.sum(scaled * unit, axis=0, keepdims=True) * (1.0 / D)
    return inverse * (scaled - mean - unit * slope)


def tree_sum(parts):
    while len(parts) > 1:
        parts = [parts[i] + parts[i + 1] for i in range(0, len(parts), 2)]
    return parts[0]


def ds(start, size, step):
    return pl.ds(pl.multiple_of(start, step), size)


def take(refs, count):
    taken = refs[:count]
    del refs[:count]
    return taken


def unit(size):
    row = lax.broadcasted_iota(jnp.int32, (size, size), 0)
    column = lax.broadcasted_iota(jnp.int32, (size, size), 1)
    return (row == column).astype(f32).astype(bf16)


def head_selector(padded_axis):
    shape = (WIDE, D) if padded_axis == 0 else (D, WIDE)
    padded = lax.broadcasted_iota(jnp.int32, shape, padded_axis)
    plain = lax.broadcasted_iota(jnp.int32, shape, 1 - padded_axis)
    inside = padded & (SLOT - 1)
    same = jnp.logical_and(plain == HEAD * (padded >> 5) + inside, inside < HEAD)
    return same.astype(f32).astype(bf16)


def pair_selector(offset, padded_axis):
    shape = (2 * WIDE, D) if padded_axis == 0 else (D, 2 * WIDE)
    padded = lax.broadcasted_iota(jnp.int32, shape, padded_axis)
    plain = lax.broadcasted_iota(jnp.int32, shape, 1 - padded_axis)
    inside = (padded & (2 * SLOT - 1)) - offset
    same = jnp.logical_and(plain == HEAD * (padded >> 6) + inside, inside >= 0)
    return jnp.logical_and(same, inside < HEAD).astype(f32).astype(bf16)


def head_rows(h):
    return slice(SLOT * h, SLOT * (h + 1))


def sample_window(step, rows_total, align):
    base = step * PAIRS
    start = jnp.minimum(base // align * align, rows_total - HALF)
    return ds(start, HALF, align), base - start


def load_sample(ref, step, fill_first):
    window, shift = sample_window(step, ref.shape[0], 16)
    rows = pltpu.roll(ref[window, :].astype(f32), lax.rem(HALF - shift, HALF), 0)
    pair_row = lax.broadcasted_iota(jnp.int32, (HALF, 2 * D), 0)
    cols = jnp.where(pair_row < PAIRS, rows, rows[0:1] if fill_first else 0.0).T
    return jnp.concatenate([cols[:D], cols[D:]], axis=1)


def store_sample(ref, step, value):
    window, shift = sample_window(step, ref.shape[0], 16 if ref.dtype == bf16 else 8)
    cols = jnp.concatenate([value[:, :HALF], value[:, HALF:]], axis=0)
    rows = pltpu.roll(cols.T, shift, 0)
    pair_row = lax.broadcasted_iota(jnp.int32, (HALF, 2 * D), 0)
    here = jnp.logical_and(pair_row >= shift, pair_row < shift + PAIRS)
    ref[window, :] = jnp.where(here, rows, ref[window, :].astype(f32)).astype(ref.dtype)


def attention_forward(normed_b, wqkv_t, wo_t, state, kh_ref, v_ref):
    e_ref, vh_ref, q_ref, k_ref, ctx_ref, rinv_ref = state
    lane = lax.broadcasted_iota(jnp.int32, (WIDE, LANES), 1)
    slot_row = lax.broadcasted_iota(jnp.int32, (WIDE, LANES), 0) & (SLOT - 1)
    real = (lane & (HALF - 1)) < PAIRS
    ones_rows = jnp.logical_or(slot_row == HEAD, slot_row == HEAD + 1).astype(f32)
    qkv = mm(wqkv_t, normed_b)
    queries = (qkv[:WIDE] * (SCALE * LOG2E)).astype(bf16)
    q_ref[...] = queries
    keys = qkv[WIDE : 2 * WIDE].astype(bf16)
    k_ref[...] = keys
    values = jnp.where(real, qkv[2 * WIDE :] + ones_rows, 0.0).astype(bf16)
    v_ref[...] = values
    for tall, ref in ((keys.T, kh_ref), (values.T, vh_ref)):
        for h in range(HEADS):
            ref[h, 0:KEYS] = tall[0:KEYS, head_rows(h)]
            ref[h, KEYS:] = tall[HALF : HALF + KEYS, head_rows(h)]

    def scores_of(h):
        return mm(kh_ref[h], q_ref[head_rows(h), :])

    scores = scores_of(0)
    for h in range(HEADS):
        rows = head_rows(h)
        ahead = scores_of(h + 1) if h + 1 < HEADS else None
        top = jnp.max(scores, axis=0, keepdims=True)
        weights = jnp.exp2(scores - top).astype(bf16)
        e_ref[0 : 2 * KEYS, LANES * h : LANES * (h + 1)] = weights
        out = mm(v_ref[rows, 0:KEYS], weights[0:KEYS]) + mm(
            v_ref[rows, HALF : HALF + KEYS], weights[KEYS:]
        )
        inverse = 1.0 / out[HEAD : HEAD + 1]
        rinv_ref[h : h + 1, :] = inverse
        ctx_ref[rows, :] = out * inverse
        scores = ahead
    return mm(wo_t, ctx_ref[...].astype(bf16))


def attention_backward(grad_b, normed_b, wo, wq, wvk, state, work, sums):
    e_ref, vh_ref, q_ref, k_ref, ctx_ref, rinv_ref = state
    pair_ref, block_ref, dq_ref, dvk_ref = work
    d_wq, d_wvk, d_wo = sums
    group = HEADS // 2
    head_row = lax.broadcasted_iota(jnp.int32, (SLOT, LANES), 0)
    lane_head = lax.broadcasted_iota(jnp.int32, (LANES, 2 * SLOT * group), 1) // (2 * SLOT)
    key_row = lax.broadcasted_iota(jnp.int32, (2 * KEYS, 2 * SLOT * group), 0)
    real_key = jnp.where(key_row < KEYS, key_row, key_row - KEYS) < PAIRS
    in_pair = lax.broadcasted_iota(jnp.int32, (2 * KEYS, 2 * SLOT * group), 1) & (2 * SLOT - 1)

    d_wo[...] += mm_nt(ctx_ref[...].astype(bf16), grad_b)
    d_context = mm(wo, grad_b)
    for h in range(HEADS):
        rows = head_rows(h)
        grad = (d_context[rows] * rinv_ref[h : h + 1, :]).astype(bf16).astype(f32)
        dot = -jnp.sum(grad[:HEAD] * ctx_ref[rows, :][:HEAD], axis=0, keepdims=True)
        dot_high = dot.astype(bf16).astype(f32)
        grad = jnp.where(head_row == HEAD, dot_high, grad)
        grad = jnp.where(head_row == HEAD + 1, dot - dot_high, grad)
        pair_ref[2 * SLOT * h : 2 * SLOT * h + SLOT, :] = grad.astype(bf16)
        pair_ref[2 * SLOT * h + SLOT : 2 * SLOT * (h + 1), :] = q_ref[rows, :]
    tall = pair_ref[...].T
    for h in range(HEADS):
        part = tall[:, WIDE * (h // group) : WIDE * (h // group + 1)]
        block_ref[LANES * h : LANES * (h + 1), :] = jnp.where(
            lane_head == h % group, part, jnp.zeros_like(part)
        )

    for h in range(HEADS + 1):
        if h < HEADS:
            lanes = slice(LANES * h, LANES * (h + 1))
            grad_probs = mm(vh_ref[h], pair_ref[2 * SLOT * h : 2 * SLOT * h + SLOT, :])
            e_ref[2 * KEYS :, lanes] = e_ref[0 : 2 * KEYS, lanes] * grad_probs.astype(bf16)
        if h > 0:
            rows = head_rows(h - 1)
            lanes = slice(LANES * (h - 1), LANES * h)
            dq = mm(k_ref[rows, 0:KEYS], e_ref[2 * KEYS : 3 * KEYS, lanes]) + mm(
                k_ref[rows, HALF : HALF + KEYS], e_ref[3 * KEYS :, lanes]
            )
            dq_ref[rows, :] = (dq * SCALE).astype(bf16)
    for g in range(2):
        here = slice(group * LANES * g, group * LANES * (g + 1))
        both = mm(e_ref[:, here], block_ref[here, :])
        dv = jnp.where(real_key, both[: 2 * KEYS], 0.0)
        dk = both[2 * KEYS :] * (1.0 / LOG2E)
        dvk = jnp.where(in_pair < SLOT, dv, dk).astype(bf16)
        for half in range(2):
            there = slice(half * HALF, half * HALF + KEYS)
            dvk_ref[there, WIDE * g : WIDE * (g + 1)] = dvk[half * KEYS : (half + 1) * KEYS]
    d_wq[...] += mm_nt(normed_b, dq_ref[...])
    d_wvk[...] += mm(normed_b, dvk_ref[...])
    return mm(wq, dq_ref[...]) + mm_nt(wvk, dvk_ref[...])


def resplit(sums):
    high = sums.astype(bf16).astype(f32)
    return jnp.concatenate([high, sums - high], axis=0).astype(bf16)


def finish_attention(d_attn, sums):
    tall, wide = head_selector(0), head_selector(1)
    for layer in range(LAYERS):
        d_wq, d_wvk, d_wo = sums[layer]
        mixed = d_wvk[...].astype(bf16)
        base = 4 * layer * D
        d_attn[base : base + D, :] = mm(d_wq[...].astype(bf16), tall)
        d_attn[base + D : base + 2 * D, :] = mm(mixed, pair_selector(SLOT, 0))
        d_attn[base + 2 * D : base + 3 * D, :] = mm(mixed, pair_selector(0, 0))
        d_attn[base + 3 * D : base + 4 * D, :] = mm(wide, d_wo[...].astype(bf16))


def finish_norms(d_norm):
    sums = [jnp.sum(d_norm[j].T, axis=0, keepdims=True) for j in range(2 * NORMS)]
    return jnp.concatenate(sums + [jnp.zeros((8 - 2 * NORMS, D), f32)], axis=0)


def pack_gradients(outs, me, parts, d_attn, d_win, d_wout, norms):
    each, upper = ATTN_ROWS // parts, parts // GROUP
    norms = resplit(norms)
    for t, out in enumerate(outs):
        for j, k in enumerate(NEAR):
            kind = out.dtype
            low = (me % GROUP) ^ k ^ (TWIN * t)
            quarter = low // 2
            half = k % 2
            for u in range(upper):
                rows = d_attn[ds((u * GROUP + low) * each, each, each), :]
                out[j, u * each : (u + 1) * each, 0:D] = rows.astype(kind)
            first = (quarter // 2) * FF + half * FFH + (quarter % 2) * WOUT_PART
            out[j, OFF_WOUT:OFF_NORM, 0:D] = d_wout[ds(first, WOUT_PART, WOUT_PART), :].astype(kind)
            out[j, OFF_NORM:OFF_WIN, 0:D] = norms.astype(kind)
            rows = d_win[ds(quarter * WIN_PART, WIN_PART, WIN_PART), half * FF : (half + 1) * FF]
            out[j, OFF_WIN:PAY_ROWS, :] = rows.astype(kind)


STATE = [
    ((4 * KEYS, HEADS * LANES), bf16),
    ((HEADS, 2 * KEYS, SLOT), bf16),
    ((WIDE, LANES), bf16),
    ((WIDE, LANES), bf16),
    ((WIDE, LANES), f32),
    ((HEADS, LANES), f32),
]
WORK = [
    ((2 * WIDE, LANES), bf16),
    ((HEADS * LANES, WIDE), bf16),
    ((WIDE, LANES), bf16),
    ((LANES, 2 * WIDE), bf16),
]
SUMS = [((D, WIDE), f32), ((D, 2 * WIDE), f32), ((WIDE, D), f32)]
GRADS = [
    *SUMS,
    *SUMS,
    ((LAYERS * D, 2 * FF), f32),
    ((LAYERS * FF, D), f32),
    ((2 * NORMS, D, 128), f32),
    ((ATTN_ROWS, D), f32),
]
SCRATCH = [
    ((LAYERS, 3 * WIDE, D), bf16),
    ((LAYERS, D, WIDE), bf16),
    ((LAYERS, D, 2 * WIDE), bf16),
    ((LAYERS, D, WIDE), bf16),
    ((LAYERS, WIDE, D), bf16),
    ((LAYERS, 2 * FF, D), bf16),
    ((LAYERS, D, 2 * FF), bf16),
    ((LAYERS, D, FF), bf16),
    ((LAYERS, FF, D), bf16),
    ((2 * NORMS, D, 128), f32),
    ((ATTN_ROWS, D), bf16),
    *GRADS,
    *STATE,
    *STATE,
    *WORK,
    ((HEADS, 2 * KEYS, SLOT), bf16),
    ((WIDE, LANES), bf16),
    ((LAYERS, 2 * FF, LANES), f32),
    ((2 * LAYERS * D, FFH), f32),
]


def main_kernel(parts, attn_diffs, *refs):
    refs = list(refs)
    me_ref, x_ref, g_ref, norm_ref, win_own, win_other, wout_own, wout_other = take(refs, 8)
    attn_refs = take(refs, len(attn_diffs) if attn_diffs else 1)
    res_ref, ig_ref = take(refs, 2)
    outs = take(refs, 2 if attn_diffs else 4)
    wqkv_t, wq, wvk, wo_t, wo, win_t, win, wout_t, wout, norm_t, attn_ref = take(refs, 11)
    sums = (take(refs, 3), take(refs, 3))
    d_win, d_wout, d_norm, d_attn = take(refs, 4)
    states = (take(refs, len(STATE)), take(refs, len(STATE)))
    work = take(refs, len(WORK))
    kh_ref, v_ref, mixed_ref, win_rows = refs
    dvk_ref = work[-1]
    step = pl.program_id(0)

    @pl.when(step == 0)
    def _():
        for ref in (*sums[0], *sums[1], d_win, d_wout, d_norm, dvk_ref):
            ref[...] = jnp.zeros_like(ref)
        if attn_diffs:
            me = me_ref[0]
            for ref, diffs in zip(attn_refs, attn_diffs, strict=True):
                each = ref.shape[1]
                for i, diff in enumerate(diffs):
                    attn_ref[ds((me ^ diff) * each, each, each), :] = ref[i]
        else:
            attn_ref[...] = attn_refs[0][...]
        norms = [norm_ref[i] for i in range(NORMS)]
        turned = jnp.concatenate(norms + [jnp.zeros((8 - 2 * NORMS, D), f32)], axis=0).T
        for i in range(2 * NORMS):
            norm_t[i] = jnp.broadcast_to(turned[:, i : i + 1], (D, 128))
        tall, wide = head_selector(0), head_selector(1)
        for layer in range(LAYERS):
            for j in range(4):
                base = (4 * layer + j) * D
                matrix = attn_ref[base : base + D, :]
                if j < 3:
                    wqkv_t[layer, j * WIDE : (j + 1) * WIDE, :] = mm_nt(tall, matrix).astype(bf16)
                if j == 0:
                    wq[layer] = mm(matrix, wide).astype(bf16)
                elif j == 1:
                    turned_keys = mm(matrix, pair_selector(SLOT, 1))
                elif j == 2:
                    wvk[layer] = (turned_keys + mm(matrix, pair_selector(0, 1))).astype(bf16)
                else:
                    padded = mm(tall, matrix).astype(bf16)
                    wo[layer] = padded
                    wo_t[layer] = mm_nt(unit(D), padded).astype(bf16)
        for p, (w1, w2) in enumerate(((win_own, wout_own), (win_other, wout_other))):
            win_rows[...] = w1[...].astype(f32)
            for layer in range(LAYERS):
                for g in range(2):
                    part = win_rows[pl.ds(2 * layer * D + g, D, stride=2), :].astype(bf16)
                    here = slice(p * FF + g * FFH, p * FF + (g + 1) * FFH)
                    win[layer, :, here] = part
                    win_t[layer, here, :] = mm_nt(unit(FFH), part).astype(bf16)
                wout_t[layer, :, p * FFH : (p + 1) * FFH] = w2[layer]
                wout[layer, p * FFH : (p + 1) * FFH, :] = mm_nt(unit(FFH), w2[layer]).astype(bf16)

    def add_norm(index, grad, unit):
        d_norm[2 * index] += fold_lanes(grad * unit)
        d_norm[2 * index + 1] += fold_lanes(grad)

    def gain_of(index):
        return jnp.concatenate([norm_t[2 * index]] * (LANES // 128), axis=1)

    def shift_of(index):
        return jnp.concatenate([norm_t[2 * index + 1]] * (LANES // 128), axis=1)

    kept = []
    normed_b = x_ref[0]
    stream = normed_b.astype(f32)
    unit_a = inv_a = None
    for layer in range(LAYERS):
        if layer > 0:
            normed, unit_a, inv_a = norm_forward(stream, gain_of(2 * layer - 1), shift_of(2 * layer - 1))
            normed_b = normed.astype(bf16)
        stream = stream + attention_forward(
            normed_b, wqkv_t[layer], wo_t[layer], states[layer], kh_ref, v_ref
        )
        normed, unit_f, inv_f = norm_forward(stream, gain_of(2 * layer), shift_of(2 * layer))
        ffn_b = normed.astype(bf16)
        mixed = mm(win_t[layer], ffn_b)
        mixed_ref[layer] = mixed
        hidden = []
        for p in range(2):
            value = mixed[FF * p : FF * p + FFH]
            gate = mixed[FF * p + FFH : FF * (p + 1)]
            hidden.append((value * (gate * sigmoid(gate))).astype(bf16))
        hidden = jnp.concatenate(hidden, axis=0)
        stream = stream + mm(wout_t[layer], hidden)
        kept.append((normed_b, unit_a, inv_a, ffn_b, unit_f, inv_f, hidden))
    res_ref[0] = stream.astype(bf16)

    grad = g_ref[0].astype(f32)
    for layer in reversed(range(LAYERS)):
        normed_b, unit_a, inv_a, ffn_b, unit_f, inv_f, hidden = kept[layer]
        grad_b = grad.astype(bf16)
        d_wout[FF * layer : FF * (layer + 1), :] += mm_nt(hidden, grad_b)
        d_hidden = mm(wout[layer], grad_b)
        d_mixed = []
        for p in range(2):
            value = mixed_ref[layer, FF * p : FF * p + FFH]
            gate = mixed_ref[layer, FF * p + FFH : FF * (p + 1)]
            part = d_hidden[FFH * p : FFH * (p + 1)]
            sig = sigmoid(gate)
            d_mixed.append((part * (gate * sig)).astype(bf16))
            d_mixed.append((part * value * sig * (1.0 + gate * (1.0 - sig))).astype(bf16))
        d_mixed = jnp.concatenate(d_mixed, axis=0)
        d_win[D * layer : D * (layer + 1), :] += mm_nt(ffn_b, d_mixed)
        d_normed = mm(win[layer], d_mixed)
        add_norm(2 * layer, d_normed, unit_f)
        grad = grad + norm_backward(d_normed, unit_f, inv_f, gain_of(2 * layer))
        d_att = attention_backward(
            grad.astype(bf16), normed_b, wo[layer], wq[layer], wvk[layer], states[layer], work, sums[layer]
        )
        if layer > 0:
            add_norm(2 * layer - 1, d_att, unit_a)
            grad = grad + norm_backward(d_att, unit_a, inv_a, gain_of(2 * layer - 1))
        else:
            grad = grad + d_att
    ig_ref[0] = grad

    @pl.when(step == pl.num_programs(0) - 1)
    def _():
        finish_attention(d_attn, sums)
        norms = finish_norms(d_norm)
        if attn_diffs:
            pack_gradients(outs, me_ref[0], parts, d_attn, d_win, d_wout, norms)
        else:
            for out, value in zip(outs, (d_attn[...], d_win[...], d_wout[...], norms), strict=True):
                out[...] = value


VMEM = pl.BlockSpec(memory_space=pltpu.VMEM)
SMEM = pl.BlockSpec(memory_space=pltpu.SMEM)


def shapes_of(pairs):
    return [jax.ShapeDtypeStruct(*pair) for pair in pairs]


def vmem_of(pairs):
    return [pltpu.VMEM(*pair) for pair in pairs]


def per_sample():
    return pl.BlockSpec((1, D, LANES), lambda i: (i, 0, 0))


def to_columns(rows, fill_first):
    samples = rows.shape[0] // PAIRS

    def body(rows_ref, out_ref):
        out_ref[0] = load_sample(rows_ref, pl.program_id(0), fill_first).astype(bf16)

    return pl.pallas_call(
        body,
        grid=(samples,),
        in_specs=[VMEM],
        out_specs=per_sample(),
        out_shape=jax.ShapeDtypeStruct((samples, D, LANES), bf16),
        compiler_params=pltpu.CompilerParams(vmem_limit_bytes=32 * 1024 * 1024),
    )(rows)


def to_rows(columns):
    samples = columns.shape[0]

    def body(columns_ref, out_ref):
        store_sample(out_ref, pl.program_id(0), columns_ref[0].astype(f32))

    return pl.pallas_call(
        body,
        grid=(samples,),
        in_specs=[per_sample()],
        out_specs=VMEM,
        out_shape=jax.ShapeDtypeStruct((samples * PAIRS, 2 * D), columns.dtype),
        compiler_params=pltpu.CompilerParams(vmem_limit_bytes=32 * 1024 * 1024),
    )(columns)


def run_main(me, tokens, cotangent, norm_params, ffn, attn_parts, parts, attn_diffs):
    samples = tokens.shape[0]
    inputs = (norm_params, *ffn, *attn_parts)
    if attn_diffs:
        grads = [((len(NEAR), PAY_ROWS, 2 * FFH), bf16)] * 2
    else:
        grads = [((ATTN_ROWS, D), f32), GRADS[6], GRADS[7], ((8, D), f32)]

    def body(*refs):
        main_kernel(parts, attn_diffs, *refs)

    out_shape = [((samples, D, LANES), bf16), ((samples, D, LANES), f32), *grads]
    res, ig, *grads = pl.pallas_call(
        body,
        grid=(samples,),
        in_specs=[SMEM, per_sample(), per_sample()] + [VMEM] * len(inputs),
        out_specs=[per_sample(), per_sample()] + [VMEM] * len(grads),
        out_shape=shapes_of(out_shape),
        scratch_shapes=vmem_of(SCRATCH),
        compiler_params=pltpu.CompilerParams(
            dimension_semantics=("arbitrary",), vmem_limit_bytes=VMEM_BYTES
        ),
        cost_estimate=pl.CostEstimate(
            flops=samples * 5_000_000_000, bytes_accessed=20_000_000, transcendentals=0
        ),
    )(me, tokens, cotangent, *inputs)
    return res, ig, grads


def small_kernel(body, out_shape, *inputs, scratch=()):
    return pl.pallas_call(
        body,
        in_specs=[SMEM] + [VMEM] * (len(inputs) - 1),
        out_specs=[VMEM] * len(out_shape),
        out_shape=shapes_of(out_shape),
        scratch_shapes=vmem_of(scratch),
        compiler_params=pltpu.CompilerParams(vmem_limit_bytes=32 * 1024 * 1024),
    )(*inputs)


class Exchange:
    def __init__(self, me, parts):
        self.me = me
        self.parts = parts
        self.upper = parts // GROUP
        self.each = ATTN_ROWS // parts
        self.bits = [1 << i for i in range(self.upper.bit_length() - 1)]

    def swap(self, value, k):
        return lax.ppermute(value, AXES, [(i, i ^ k) for i in range(self.parts)])

    def stack(self, blocks):
        size, kind = blocks[0].shape, blocks[0].dtype
        count = math.prod(size[:-2])

        def body(me_ref, *refs):
            ins, out = refs[:-1], refs[-1]
            for i, ref in enumerate(ins):
                if len(size) == 2:
                    out[i] = ref[...]
                else:
                    out[i * count : (i + 1) * count] = ref[...]

        shape = (len(blocks) * count, *size[-2:])
        return small_kernel(body, [(shape, kind)], self.me, *blocks)[0]

    def gather(self, rows, beside_rest, beside_plane):
        far = [GROUP * u for u in range(self.upper)]
        landed = [rows] + [self.swap(rows, k) for k in far[1:]]
        landed, beside_rest = lax.optimization_barrier((landed, beside_rest))
        column = self.stack(landed)
        landed = [column] + [self.swap(column, k) for k in NEAR[1:]]
        landed, beside_plane = lax.optimization_barrier((landed, beside_plane))
        plane = self.stack(landed)
        diffs = [k ^ u for k in NEAR for u in far]
        parts, diffs = [plane, self.swap(plane, TWIN)], [diffs, [d ^ TWIN for d in diffs]]
        return parts, diffs, beside_rest, beside_plane

    def twins(self, mine, theirs):
        def body(me_ref, mine, theirs, *outs):
            for j, out in enumerate(outs):
                total = mine[j].astype(f32) + theirs[j].astype(f32)
                out[0:OFF_NORM] = total[0:OFF_NORM].astype(out.dtype)
                sums = total[OFF_NORM : OFF_NORM + 8] + total[OFF_NORM + 8 : OFF_WIN]
                out[OFF_NORM:OFF_WIN] = resplit(sums).astype(out.dtype)
                out[OFF_WIN:] = total[OFF_WIN:].astype(out.dtype)

        shape = (PAY_ROWS, 2 * FFH)
        shapes = [(shape, f32)] + [(shape, bf16)] * (len(NEAR) - 1)
        return small_kernel(body, shapes, self.me, mine, theirs)

    def across_plane(self, pieces):
        return [pieces[0]] + [self.swap(piece, k) for piece, k in zip(pieces[1:], NEAR[1:], strict=True)]

    def emit(self, total, blocks, at, keep, send):
        half = len(blocks) // 2
        each = self.each
        for out, rows in ((keep, blocks[:half]), (send, blocks[half:])):
            for i, row in enumerate(rows):
                out[i * each : (i + 1) * each, :] = total[ds(row, each, 8), :].astype(out.dtype)
        first = half * each
        last = at + OFF_NORM - OFF_WOUT
        norm = resplit(total[last : last + 8, :] + total[last + 8 : last + 16, :])
        rest = [
            total[at:last, :].astype(bf16),
            norm,
            total[last + 16 : at + PAY_ROWS - OFF_WOUT, :].astype(bf16),
        ]
        for out in (keep, send):
            row = first
            for part in rest:
                out[row : row + part.shape[0], :] = part.astype(out.dtype)
                row += part.shape[0]

    def stage_shapes(self, blocks):
        shape = (blocks * self.each + PAY_ROWS - OFF_WOUT, 2 * FFH)
        return [(shape, f32), (shape, bf16)]

    def after_plane(self, landed):
        def body(me_ref, *refs):
            ins, (keep, send, total) = refs[: len(NEAR)], refs[len(NEAR) :]
            total[...] = tree_sum([r[...].astype(f32) for r in ins])
            mine = me_ref[0] // GROUP
            order = [r for r in range(self.upper) if not r & 1] + [r for r in range(self.upper) if r & 1]
            self.emit(total, [(mine ^ r) * self.each for r in order], OFF_WOUT, keep, send)

        scratch = [((PAY_ROWS, 2 * FFH), f32)]
        return small_kernel(body, self.stage_shapes(self.upper // 2), self.me, *landed, scratch=scratch)

    def after_bit(self, mine, theirs, blocks):
        def body(me_ref, mine, theirs, keep, send, total):
            total[...] = mine[...] + theirs[...].astype(f32)
            self.emit(total, [i * self.each for i in range(blocks)], blocks * self.each, keep, send)

        (shape, _), _ = self.stage_shapes(blocks)
        return small_kernel(
            body, self.stage_shapes(blocks // 2), self.me, mine, theirs, scratch=[(shape, f32)]
        )

    def after_rest(self, mine, theirs):
        each = self.each
        at_norm = each + WOUT_PART
        ffn_rows = WOUT_PART + WIN_PART

        def body(me_ref, mine, theirs, attn, norm, ffn):
            total = mine[...] + theirs[...].astype(f32)
            attn[...] = total[0:each, 0:D]
            norm[...] = total[at_norm : at_norm + 8, 0:D] + total[at_norm + 8 : at_norm + 16, 0:D]
            ffn[0, 0:WOUT_PART, :] = total[each:at_norm, :].astype(bf16)
            ffn[0, WOUT_PART:, :] = total[at_norm + 16 :, :].astype(bf16)

        shapes = [((each, D), f32), ((8, D), f32), ((1, ffn_rows, 2 * FFH), bf16)]
        return small_kernel(body, shapes, self.me, mine, theirs)

    def spread(self, ffn):
        block = self.stack([ffn, self.swap(ffn, 4)])
        theirs = self.swap(block, TWIN)

        def body(me_ref, mine, theirs, win, wout, rows):
            for t, ref in enumerate((mine, theirs)):
                for i in range(2):
                    quarter = ((me_ref[0] % GROUP) ^ (4 * i) ^ (TWIN * t)) // 2
                    part = ref[i].astype(f32)
                    rows[ds(quarter * WOUT_PART, WOUT_PART, WOUT_PART), :] = part[:WOUT_PART, 0:D]
                    for g in range(2):
                        there = pl.ds(2 * WIN_PART * quarter + g, WIN_PART, stride=2)
                        win[there, :] = part[WOUT_PART:, FFH * g : FFH * (g + 1)]
            for layer in range(LAYERS):
                wout[layer] = rows[FFH * layer : FFH * (layer + 1), :].T

        shapes = [((2 * LAYERS * D, FFH), f32), ((LAYERS, D, FFH), f32)]
        scratch = [((LAYERS * FFH, D), f32)]
        return small_kernel(body, shapes, self.me, block, theirs, scratch=scratch)

    def sum_all(self, keep, send, res, ig):
        landed = self.across_plane(self.twins(keep, self.swap(send, TWIN)))
        landed, res = lax.optimization_barrier((landed, to_rows(res)))
        keep, send = self.after_plane(landed)
        blocks = self.upper // 2
        for bit in self.bits[:-1]:
            keep, send = self.after_bit(keep, self.swap(send, GROUP * bit), blocks)
            blocks //= 2
        theirs = self.swap(send, GROUP * self.bits[-1])
        theirs, ig = lax.optimization_barrier((theirs, to_rows(ig)))
        attn, norm, ffn = self.after_rest(keep, theirs)
        return res, ig, attn, norm, *self.spread(ffn)


def on_device(devices, tokens, attn_weights, norm_params, w_in, w_out, cotangent):
    each = attn_weights.shape[0]
    me = (lax.axis_index("dp") * 2 + lax.axis_index("narrow")).astype(jnp.int32).reshape(1)
    staged = devices % (2 * GROUP) == 0 and each % 16 == 0
    x_t = to_columns(tokens, True)
    g_t = to_columns(cotangent, False)
    swap_halves = [(0, 1), (1, 0)]
    w_in = w_in.reshape(2 * LAYERS * D, FFH)
    w_out = w_out.transpose(0, 2, 1)
    w_in_other = lax.ppermute(w_in, "narrow", swap_halves)
    w_out_other = lax.ppermute(w_out, "narrow", swap_halves)
    ffn = (w_in, w_in_other, w_out, w_out_other)
    if not staged:
        attn_all = lax.all_gather(attn_weights, AXES, axis=0, tiled=True)
        res, ig, grads = run_main(me, x_t, g_t, norm_params, ffn, (attn_all,), devices, None)
        res, ig = to_rows(res), to_rows(ig)
        d_attn, d_win, d_wout, sums = grads
        attn = lax.psum_scatter(d_attn, AXES, scatter_dimension=0, tiled=True)
        norm = lax.psum(sums, AXES)
        d_wout = d_wout.reshape(LAYERS, FF, D)
        own_in, other_in = d_win[:, :FF], d_win[:, FF:]
        own_out, other_out = d_wout[:, :FFH], d_wout[:, FFH:]
        win = lax.psum(own_in + lax.ppermute(other_in, "narrow", swap_halves), "dp")
        wout = lax.psum(own_out + lax.ppermute(other_out, "narrow", swap_halves), "dp")
        wout = wout.transpose(0, 2, 1)
    else:
        ex = Exchange(me, devices)
        attn_parts, attn_diffs, (x_t, *others), g_t = ex.gather(
            attn_weights, (x_t, w_in_other, w_out_other), g_t
        )
        ffn = (w_in, others[0], w_out, others[1])
        res, ig, grads = run_main(me, x_t, g_t, norm_params, ffn, attn_parts, devices, attn_diffs)
        res, ig, attn, norm, win, wout = ex.sum_all(*grads, res, ig)
    return (
        res,
        ig,
        attn,
        norm[: 2 * NORMS].reshape(norm_params.shape),
        win.reshape(LAYERS, D, 2, FFH),
        wout.transpose(0, 2, 1),
    )


def solution(mesh):
    rows = P(("dp", "narrow"), None)
    hidden_in = P(None, None, None, "narrow")
    hidden_out = P(None, "narrow", None)
    devices = mesh.shape["dp"] * mesh.shape["narrow"]

    def per_device(*args):
        return on_device(devices, *args)

    return jax.shard_map(
        per_device,
        mesh=mesh,
        in_specs=(rows, rows, P(), hidden_in, hidden_out, rows),
        out_specs=(rows, rows, rows, P(), hidden_in, hidden_out),
        check_vma=False,
    )
```

profile of v0, /device:TPU:0, one launch (start us, length us, event | category | flops | bytes accessed | tf_op | source)
XLA Modules:
  0.0 197.1 jit_solution(8368841304071483490)
XLA Ops:
  0.6 3.0 %collective-permute-start.3 = (bf16[768,128]{1,0:T(8,128)(2,1)}, bf16[768,128]{1,0:T(8,128)(2,1)S(1)}, u32[]{:S(2)}, u32[]{:S(2)}) collective-permute-start(bf16[768,128]{1,0:T(8,128)(2,1)} %bitcast.8), channel_id=1, source_target_pairs={{0,1},{1,0},{2,3},{3,2},{4,5},{5,4},{6,7},{7,6},{8,9},{9,8},{10,11... | collective-permute-start | bytes 589832 | tf_op jit(solution)/shard_map/ppermute | solution.py:703
  3.7 3.0 %collective-permute-start.1 = (bf16[48,192]{1,0:T(8,128)(2,1)}, bf16[48,192]{1,0:T(8,128)(2,1)S(1)}, u32[]{:S(2)}, u32[]{:S(2)}) collective-permute-start(bf16[48,192]{1,0:T(8,128)(2,1)} %refs_0_), channel_id=1, source_target_pairs={{0,16},{1,17},{2,18},{3,19},{4,20},{5,21},{6,22},{7,23},{8,24},{9,... | collective-permute-start | bytes 55304 | tf_op jit(solution)/shard_map/ppermute | solution.py:555
  6.8 1.6 collective-permute-start
  8.3 1.4 copy-done.4
  9.7 2.0 %shard_map.109.refs_1_ = bf16[8,192,512]{2,1,0:T(8,128)(2,1)S(1)} custom-call(bf16[1904,384]{1,0:T(8,128)(2,1)S(1)} %copy-done.4), custom_call_target="tpu_custom_call" | custom-call | tf_op jit(solution)/shard_map/pallas_call | solution.py:480
  11.8 1.1 copy-done.1
  12.9 1.3 collective-permute-done.2.refs_3_
  14.2 2.5 %collective-permute-start.7 = (bf16[4,48,192]{2,1,0:T(8,128)(2,1)S(1)}, bf16[4,48,192]{2,1,0:T(8,128)(2,1)S(1)}, u32[]{:S(2)}, u32[]{:S(2)}) collective-permute-start(bf16[4,48,192]{2,1,0:T(8,128)(2,1)S(1)} %shard_map.110.refs_0_), channel_id=1, source_target_pairs={{0,5},{1,4},{2,7},{3,6},{4,1},{5,0},{6,3},{7,2},{8,13},{9,12},{10,... | collective-permute-start | bytes 221192 | tf_op jit(solution)/shard_map/ppermute | solution.py:555
  17.8 2.0 %shard_map.111.refs_2_ = bf16[8,192,512]{2,1,0:T(8,128)(2,1)S(1)} custom-call(bf16[1904,384]{1,0:T(8,128)(2,1)S(1)} %copy-done.5), custom_call_target="tpu_custom_call" | custom-call | tf_op jit(solution)/shard_map/pallas_call | solution.py:480
  19.8 1.1 copy-done.3
  22.0 1.7 collective-permute-done.8.refs_9_
  24.4 137.5 %shard_map.113 = (bf16[8,192,512]{2,1,0:T(8,128)(2,1)}, f32[8,192,512]{2,1,0:T(8,128)}, bf16[4,368,256]{2,1,0:T(8,128)(2,1)}, bf16[4,368,256]{2,1,0:T(8,128)(2,1)}) custom-call(s32[1]{0:T(128)} %bitcast.me_ref.refs_0_, bf16[8,192,512]{2,1,0:T(8,128)(2,1)} %copy-done.1, bf16[8,192,512]{2,1,0:T(8,128)(2,1)} %copy-done.3, f32[3,2,192]{2,1,0:T(2,128)} %refs_3_.1, ...), custom_call_target="tpu_custom_call" | custom-call | flops 40000000000 | bytes 20000000 | tf_op jit(solution)/shard_map/pallas_call | solution.py:518
  162.2 2.3 %collective-permute-done.9.theirs = bf16[4,368,256]{2,1,0:T(8,128)(2,1)S(1)} collective-permute-done((bf16[4,368,256]{2,1,0:T(8,128)(2,1)}, bf16[4,368,256]{2,1,0:T(8,128)(2,1)S(1)}, u32[]{:S(2)}, u32[]{:S(2)}) %collective-permute-start.9) | collective-permute-done | bytes 753696 | tf_op jit(solution)/shard_map/ppermute | solution.py:555
  164.5 1.1 copy-done.6
  166.5 1.5 collective-permute-start.11
  168.0 1.3 collective-permute-start.12
  169.3 1.4 copy-done.2
  170.8 4.0 %shard_map.115 = bf16[1904,384]{1,0:T(8,128)(2,1)} custom-call(bf16[8,192,512]{2,1,0:T(8,128)(2,1)S(1)} %copy-done.2), custom_call_target="tpu_custom_call" | custom-call | tf_op jit(solution)/shard_map/pallas_call | solution.py:496
  174.8 1.3 collective-permute-done.11.refs_2_
  176.1 1.5 collective-permute-done.12.refs_3_
  177.9 5.0 %collective-permute-done.13.theirs = bf16[272,256]{1,0:T(8,128)(2,1)S(1)} collective-permute-done((bf16[272,256]{1,0:T(8,128)(2,1)S(1)}, bf16[272,256]{1,0:T(8,128)(2,1)S(1)}, u32[]{:S(2)}, u32[]{:S(2)}) %collective-permute-start.13) | collective-permute-done | bytes 139296 | tf_op jit(solution)/shard_map/ppermute | solution.py:555
  183.0 1.3 collective-permute-start.14
  184.3 4.5 %shard_map.118 = f32[1904,384]{1,0:T(8,128)} custom-call(f32[8,192,512]{2,1,0:T(8,128)S(1)} %copy-done), custom_call_target="tpu_custom_call" | custom-call | tf_op jit(solution)/shard_map/pallas_call | solution.py:496
  191.2 3.5 %collective-permute-done.15.refs_1_ = bf16[1,160,256]{2,1,0:T(8,128)(2,1)S(1)} collective-permute-done((bf16[1,160,256]{2,1,0:T(8,128)(2,1)S(1)}, bf16[1,160,256]{2,1,0:T(8,128)(2,1)S(1)}, u32[]{:S(2)}, u32[]{:S(2)}) %collective-permute-start.15) | collective-permute-done | bytes 81952 | tf_op jit(solution)/shard_map/ppermute | solution.py:555
  (48 shorter events, 9.0 us)
Async XLA Ops:
  0.6 13.5 %collective-permute-start.3 = (bf16[768,128]{1,0:T(8,128)(2,1)}, bf16[768,128]{1,0:T(8,128)(2,1)S(1)}, u32[]{:S(2)}, u32[]{:S(2)}) collective-permute-start(bf16[768,128]{1,0:T(8,128)(2,1)} %bitcast.8), channel_id=1, source_target_pairs={{0,1},{1,0},{2,3},{3,2},{4,5},{5,4},{6,7},{7,6},{8,9},{9,8},{10,11... | collective-permute-start | bytes 589832 | tf_op jit(solution)/shard_map/ppermute | solution.py:703
  3.6 10.5 %collective-permute-start.4 = (bf16[2,192,128]{2,1,0:T(8,128)(2,1)}, bf16[2,192,128]{2,1,0:T(8,128)(2,1)S(1)}, u32[]{:S(2)}, u32[]{:S(2)}) collective-permute-start(bf16[2,192,128]{2,1,0:T(8,128)(2,1)} %bitcast.11), channel_id=1, source_target_pairs={{0,1},{1,0},{2,3},{3,2},{4,5},{5,4},{6,7},{7,6},{8,9},{9,8},{10,11... | collective-permute-start | bytes 294920 | tf_op jit(solution)/shard_map/ppermute | solution.py:704
  3.7 9.2 %collective-permute-start.1 = (bf16[48,192]{1,0:T(8,128)(2,1)}, bf16[48,192]{1,0:T(8,128)(2,1)S(1)}, u32[]{:S(2)}, u32[]{:S(2)}) collective-permute-start(bf16[48,192]{1,0:T(8,128)(2,1)} %refs_0_), channel_id=1, source_target_pairs={{0,16},{1,17},{2,18},{3,19},{4,20},{5,21},{6,22},{7,23},{8,24},{9,... | collective-permute-start | bytes 55304 | tf_op jit(solution)/shard_map/ppermute | solution.py:555
  6.8 6.2 %collective-permute-start = (bf16[48,192]{1,0:T(8,128)(2,1)}, bf16[48,192]{1,0:T(8,128)(2,1)S(1)}, u32[]{:S(2)}, u32[]{:S(2)}) collective-permute-start(bf16[48,192]{1,0:T(8,128)(2,1)} %refs_0_), channel_id=1, source_target_pairs={{0,8},{1,9},{2,10},{3,11},{4,12},{5,13},{6,14},{7,15},{8,0},{9,1},... | collective-permute-start | bytes 55304 | tf_op jit(solution)/shard_map/ppermute | solution.py:555
  8.3 5.8 %collective-permute-start.2 = (bf16[48,192]{1,0:T(8,128)(2,1)}, bf16[48,192]{1,0:T(8,128)(2,1)S(1)}, u32[]{:S(2)}, u32[]{:S(2)}) collective-permute-start(bf16[48,192]{1,0:T(8,128)(2,1)} %refs_0_), channel_id=1, source_target_pairs={{0,24},{1,25},{2,26},{3,27},{4,28},{5,29},{6,30},{7,31},{8,16},{9,... | collective-permute-start | bytes 55304 | tf_op jit(solution)/shard_map/ppermute | solution.py:555
  9.7 4.5 %copy-start.8 = (bf16[48,192]{1,0:T(8,128)(2,1)S(1)}, bf16[48,192]{1,0:T(8,128)(2,1)}, u32[]{:S(2)}) copy-start(bf16[48,192]{1,0:T(8,128)(2,1)} %refs_0_) | copy-start | bytes 55300
  9.7 8.1 %copy-start.5 = (bf16[1904,384]{1,0:T(8,128)(2,1)S(1)}, bf16[1904,384]{1,0:T(8,128)(2,1)}, u32[]{:S(2)}) copy-start(bf16[1904,384]{1,0:T(8,128)(2,1)} %rows_ref.3) | copy-start | bytes 4386820
  14.2 5.6 %copy-start.11 = (bf16[2,192,128]{2,1,0:T(8,128)(2,1)}, bf16[2,192,128]{2,1,0:T(8,128)(2,1)S(1)}, u32[]{:S(2)}) copy-start(bf16[2,192,128]{2,1,0:T(8,128)(2,1)S(1)} %collective-permute-done.4.refs_7_) | copy-start | bytes 294916
  14.2 5.6 %copy-start.10 = (bf16[768,128]{1,0:T(8,128)(2,1)}, bf16[768,128]{1,0:T(8,128)(2,1)S(1)}, u32[]{:S(2)}) copy-start(bf16[768,128]{1,0:T(8,128)(2,1)S(1)} %collective-permute-done.3.refs_5_) | copy-start | bytes 589828
  14.2 6.8 %collective-permute-start.7 = (bf16[4,48,192]{2,1,0:T(8,128)(2,1)S(1)}, bf16[4,48,192]{2,1,0:T(8,128)(2,1)S(1)}, u32[]{:S(2)}, u32[]{:S(2)}) collective-permute-start(bf16[4,48,192]{2,1,0:T(8,128)(2,1)S(1)} %shard_map.110.refs_0_), channel_id=1, source_target_pairs={{0,5},{1,4},{2,7},{3,6},{4,1},{5,0},{6,3},{7,2},{8,13},{9,12},{10,... | collective-permute-start | bytes 221192 | tf_op jit(solution)/shard_map/ppermute | solution.py:555
  16.7 4.6 %collective-permute-start.6 = (bf16[4,48,192]{2,1,0:T(8,128)(2,1)S(1)}, bf16[4,48,192]{2,1,0:T(8,128)(2,1)S(1)}, u32[]{:S(2)}, u32[]{:S(2)}) collective-permute-start(bf16[4,48,192]{2,1,0:T(8,128)(2,1)S(1)} %shard_map.110.refs_0_), channel_id=1, source_target_pairs={{0,4},{1,5},{2,6},{3,7},{4,0},{5,1},{6,2},{7,3},{8,12},{9,13},{10,... | collective-permute-start | bytes 221192 | tf_op jit(solution)/shard_map/ppermute | solution.py:555
  17.2 4.6 %collective-permute-start.5 = (bf16[4,48,192]{2,1,0:T(8,128)(2,1)S(1)}, bf16[4,48,192]{2,1,0:T(8,128)(2,1)S(1)}, u32[]{:S(2)}, u32[]{:S(2)}) collective-permute-start(bf16[4,48,192]{2,1,0:T(8,128)(2,1)S(1)} %shard_map.110.refs_0_), channel_id=1, source_target_pairs={{0,1},{1,0},{2,3},{3,2},{4,5},{5,4},{6,7},{7,6},{8,9},{9,8},{10,11... | collective-permute-start | bytes 221192 | tf_op jit(solution)/shard_map/ppermute | solution.py:555
  21.9 1.8 copy-start.7
  21.9 1.8 collective-permute-start.8
  162.0 2.5 %collective-permute-start.9 = (bf16[4,368,256]{2,1,0:T(8,128)(2,1)}, bf16[4,368,256]{2,1,0:T(8,128)(2,1)S(1)}, u32[]{:S(2)}, u32[]{:S(2)}) collective-permute-start(bf16[4,368,256]{2,1,0:T(8,128)(2,1)} %get-tuple-element.55), channel_id=1, source_target_pairs={{0,2},{1,3},{2,0},{3,1},{4,6},{5,7},{6,4},{7,5},{8,10},{9,11},{10,... | collective-permute-start | bytes 2261000 | tf_op jit(solution)/shard_map/ppermute | solution.py:555
  165.8 9.0 %collective-permute-start.10 = (bf16[368,256]{1,0:T(8,128)(2,1)S(1)}, bf16[368,256]{1,0:T(8,128)(2,1)S(1)}, u32[]{:S(2)}, u32[]{:S(2)}) collective-permute-start(bf16[368,256]{1,0:T(8,128)(2,1)S(1)} %get-tuple-element.57), channel_id=1, source_target_pairs={{0,1},{1,0},{2,3},{3,2},{4,5},{5,4},{6,7},{7,6},{8,9},{9,8},{10,11... | collective-permute-start | bytes 565256 | tf_op jit(solution)/shard_map/ppermute | solution.py:555
  166.5 9.6 %collective-permute-start.11 = (bf16[368,256]{1,0:T(8,128)(2,1)S(1)}, bf16[368,256]{1,0:T(8,128)(2,1)S(1)}, u32[]{:S(2)}, u32[]{:S(2)}) collective-permute-start(bf16[368,256]{1,0:T(8,128)(2,1)S(1)} %get-tuple-element.58), channel_id=1, source_target_pairs={{0,4},{1,5},{2,6},{3,7},{4,0},{5,1},{6,2},{7,3},{8,12},{9,13},{10,... | collective-permute-start | bytes 565256 | tf_op jit(solution)/shard_map/ppermute | solution.py:555
  168.0 9.6 %collective-permute-start.12 = (bf16[368,256]{1,0:T(8,128)(2,1)S(1)}, bf16[368,256]{1,0:T(8,128)(2,1)S(1)}, u32[]{:S(2)}, u32[]{:S(2)}) collective-permute-start(bf16[368,256]{1,0:T(8,128)(2,1)S(1)} %get-tuple-element.59), channel_id=1, source_target_pairs={{0,5},{1,4},{2,7},{3,6},{4,1},{5,0},{6,3},{7,2},{8,13},{9,12},{10,... | collective-permute-start | bytes 565256 | tf_op jit(solution)/shard_map/ppermute | solution.py:555
  169.3 1.4 copy-start.2
  170.8 13.6 %copy-start = (f32[8,192,512]{2,1,0:T(8,128)S(1)}, f32[8,192,512]{2,1,0:T(8,128)}, u32[]{:S(2)}) copy-start(f32[8,192,512]{2,1,0:T(8,128)} %get-tuple-element.69.columns_ref) | copy-start | bytes 9437188
  177.8 5.1 %collective-permute-start.13 = (bf16[272,256]{1,0:T(8,128)(2,1)S(1)}, bf16[272,256]{1,0:T(8,128)(2,1)S(1)}, u32[]{:S(2)}, u32[]{:S(2)}) collective-permute-start(bf16[272,256]{1,0:T(8,128)(2,1)S(1)} %get-tuple-element.67), channel_id=1, source_target_pairs={{0,8},{1,9},{2,10},{3,11},{4,12},{5,13},{6,14},{7,15},{8,0},{9,1},... | collective-permute-start | bytes 417800 | tf_op jit(solution)/shard_map/ppermute | solution.py:555
  183.0 6.7 %collective-permute-start.14 = (bf16[224,256]{1,0:T(8,128)(2,1)S(1)}, bf16[224,256]{1,0:T(8,128)(2,1)S(1)}, u32[]{:S(2)}, u32[]{:S(2)}) collective-permute-start(bf16[224,256]{1,0:T(8,128)(2,1)S(1)} %get-tuple-element.68), channel_id=1, source_target_pairs={{0,16},{1,17},{2,18},{3,19},{4,20},{5,21},{6,22},{7,23},{8,24},{9,... | collective-permute-start | bytes 344072 | tf_op jit(solution)/shard_map/ppermute | solution.py:555
  190.3 4.4 %collective-permute-start.15 = (bf16[1,160,256]{2,1,0:T(8,128)(2,1)S(1)}, bf16[1,160,256]{2,1,0:T(8,128)(2,1)S(1)}, u32[]{:S(2)}, u32[]{:S(2)}) collective-permute-start(bf16[1,160,256]{2,1,0:T(8,128)(2,1)S(1)} %get-tuple-element.75.refs_0_), channel_id=1, source_target_pairs={{0,4},{1,5},{2,6},{3,7},{4,0},{5,1},{6,2},{7,3},{8,12},{9,13},{10,... | collective-permute-start | bytes 245768 | tf_op jit(solution)/shard_map/ppermute | solution.py:555
  194.7 1.5 collective-permute-start.16
  (5 other events, 5.5 us)
where the time goes:
time: 197 us
  Pallas kernels  152 us (77%)
  waiting for transfers between devices  19.2 us (10%)
  starting transfers between devices  17.5 us (9%)
  local copies, waits for them, and re-layouts  7.56 us (4%)
    pallas_call x1, Pallas kernels, run_main(): pl.pallas_call(body, grid=(samples,), in_specs=[SMEM, per_sample(), per_s...  138 us
    ppermute x15, waiting for transfers between devices, swap(): return lax.ppermute(value, AXES, [(i, i ^ k) for i in range(self.parts)])  19.2 us
    ppermute x15, starting transfers between devices, swap(): return lax.ppermute(value, AXES, [(i, i ^ k) for i in range(self.parts)])  14.4 us
    pallas_call x2, Pallas kernels, to_rows(): pl.pallas_call(body, grid=(samples,), in_specs=[per_sample()], out_specs=...  8.5 us
    unnamed x24, local copies, waits for them, and re-layouts  6.96 us
    pallas_call x2, Pallas kernels, to_columns(): pl.pallas_call(body, grid=(samples,), in_specs=[VMEM], out_specs=per_samp...  4.07 us
  transfers between devices with their start and end apart: 17, of which 11 were waited for; matrix products, arithmetic and copies ran while one was open for 0% of the time, Pallas kernels for 6%

commit v1 on v0

--- a/solution.py
+++ b/solution.py
@@ -30,18 +30,23 @@
 NEAR = (0, 1, 4, 5)
 TWIN = 2
 WIN_PART = LAYERS * D // 4
+SIDE = 2 * FFH - D
 WOUT_PART = LAYERS * FFH // 4
 ATTN_PART = ATTN_ROWS // GROUP
 OFF_WOUT = ATTN_PART
 OFF_NORM = OFF_WOUT + WOUT_PART
 OFF_WIN = OFF_NORM + 16
 PAY_ROWS = OFF_WIN + WIN_PART
+PACK_WOUT = 3 * ATTN_PART // 4
+PACK_NORM = PACK_WOUT + 3 * WOUT_PART // 4
+PACK_WIN = PACK_NORM + 16
+PACK_ROWS = PACK_WIN + WIN_PART
 
 bf16 = jnp.bfloat16
 f32 = jnp.float32
 AXES = ("dp", "narrow")
 
-VMEM_BYTES = 60 * 1024 * 1024
+VMEM_BYTES = 52 * 1024 * 1024
 
 
 def mm(left, right):
@@ -261,18 +266,22 @@
     norms = resplit(norms)
     for t, out in enumerate(outs):
         for j, k in enumerate(NEAR):
-            kind = out.dtype
             low = (me % GROUP) ^ k ^ (TWIN * t)
             quarter = low // 2
             half = k % 2
-            for u in range(upper):
-                rows = d_attn[ds((u * GROUP + low) * each, each, each), :]
-                out[j, u * each : (u + 1) * each, 0:D] = rows.astype(kind)
+            attn = [d_attn[ds((u * GROUP + low) * each, each, each), :] for u in range(upper)]
             first = (quarter // 2) * FF + half * FFH + (quarter % 2) * WOUT_PART
-            out[j, OFF_WOUT:OFF_NORM, 0:D] = d_wout[ds(first, WOUT_PART, WOUT_PART), :].astype(kind)
-            out[j, OFF_NORM:OFF_WIN, 0:D] = norms.astype(kind)
-            rows = d_win[ds(quarter * WIN_PART, WIN_PART, WIN_PART), half * FF : (half + 1) * FF]
-            out[j, OFF_WIN:PAY_ROWS, :] = rows.astype(kind)
+            wout = d_wout[ds(first, WOUT_PART, WOUT_PART), :]
+            win = d_win[ds(quarter * WIN_PART, WIN_PART, WIN_PART), half * FF : (half + 1) * FF]
+            for at, value in ((0, jnp.concatenate(attn, axis=0)), (PACK_WOUT, wout)):
+                value = value.astype(bf16)
+                rows = value.shape[0] // 4
+                out[j, at : at + 3 * rows, 0:D] = value[: 3 * rows]
+                for c in range(3):
+                    part = value[3 * rows :, SIDE * c : SIDE * (c + 1)]
+                    out[j, at + rows * c : at + rows * (c + 1), D:] = part
+            out[j, PACK_NORM:PACK_WIN, 0:D] = norms
+            out[j, PACK_WIN:PACK_ROWS, :] = win.astype(bf16)
 
 
 STATE = [
@@ -507,7 +516,7 @@
     samples = tokens.shape[0]
     inputs = (norm_params, *ffn, *attn_parts)
     if attn_diffs:
-        grads = [((len(NEAR), PAY_ROWS, 2 * FFH), bf16)] * 2
+        grads = [((len(NEAR), PACK_ROWS, 2 * FFH), bf16)] * 2
     else:
         grads = [((ATTN_ROWS, D), f32), GRADS[6], GRADS[7], ((8, D), f32)]
 
@@ -585,12 +594,12 @@
         def body(me_ref, mine, theirs, *outs):
             for j, out in enumerate(outs):
                 total = mine[j].astype(f32) + theirs[j].astype(f32)
-                out[0:OFF_NORM] = total[0:OFF_NORM].astype(out.dtype)
-                sums = total[OFF_NORM : OFF_NORM + 8] + total[OFF_NORM + 8 : OFF_WIN]
-                out[OFF_NORM:OFF_WIN] = resplit(sums).astype(out.dtype)
-                out[OFF_WIN:] = total[OFF_WIN:].astype(out.dtype)
-
-        shape = (PAY_ROWS, 2 * FFH)
+                out[0:PACK_NORM] = total[0:PACK_NORM].astype(out.dtype)
+                sums = total[PACK_NORM : PACK_NORM + 8] + total[PACK_NORM + 8 : PACK_WIN]
+                out[PACK_NORM:PACK_WIN] = resplit(sums).astype(out.dtype)
+                out[PACK_WIN:] = total[PACK_WIN:].astype(out.dtype)
+
+        shape = (PACK_ROWS, 2 * FFH)
         shapes = [(shape, f32)] + [(shape, bf16)] * (len(NEAR) - 1)
         return small_kernel(body, shapes, self.me, mine, theirs)
 
@@ -623,13 +632,21 @@
 
     def after_plane(self, landed):
         def body(me_ref, *refs):
-            ins, (keep, send, total) = refs[: len(NEAR)], refs[len(NEAR) :]
-            total[...] = tree_sum([r[...].astype(f32) for r in ins])
+            ins, (keep, send, packed, total) = refs[: len(NEAR)], refs[len(NEAR) :]
+            packed[...] = tree_sum([r[...].astype(f32) for r in ins])
+            for at, to, size in ((0, 0, ATTN_PART), (PACK_WOUT, OFF_WOUT, WOUT_PART)):
+                rows = size // 4
+                total[to : to + 3 * rows, 0:D] = packed[at : at + 3 * rows, 0:D]
+                for c in range(3):
+                    part = packed[at + rows * c : at + rows * (c + 1), D:]
+                    total[to + 3 * rows : to + size, SIDE * c : SIDE * (c + 1)] = part
+            total[OFF_NORM:OFF_WIN, :] = packed[PACK_NORM:PACK_WIN, :]
+            total[OFF_WIN:, :] = packed[PACK_WIN:, :]
             mine = me_ref[0] // GROUP
             order = [r for r in range(self.upper) if not r & 1] + [r for r in range(self.upper) if r & 1]
             self.emit(total, [(mine ^ r) * self.each for r in order], OFF_WOUT, keep, send)
 
-        scratch = [((PAY_ROWS, 2 * FFH), f32)]
+        scratch = [((PACK_ROWS, 2 * FFH), f32), ((PAY_ROWS, 2 * FFH), f32)]
         return small_kernel(body, self.stage_shapes(self.upper // 2), self.me, *landed, scratch=scratch)
 
     def after_bit(self, mine, theirs, blocks):

time: 197 us -> 193 us (0.980)
    unnamed x24 -> x20, local copies, waits for them, and re-layouts: 6.96 us -> 5.1 us
  transfers between devices with their start and end apart: 17 -> 17, of which waited for: 11 -> 10; matrix products, arithmetic and copies ran while one was open for 0% -> 0% of each run, Pallas kernels for 6% -> 7%
where the time goes in v1:
time: 193 us
  Pallas kernels  151 us (78%)
  waiting for transfers between devices  17.6 us (9%)
  starting transfers between devices  17.4 us (9%)
  local copies, waits for them, and re-layouts  5.7 us (3%)
    pallas_call x1, Pallas kernels, run_main(): pl.pallas_call(body, grid=(samples,), in_specs=[SMEM, per_sample(), per_s...  137 us
    ppermute x15, waiting for transfers between devices, swap(): return lax.ppermute(value, AXES, [(i, i ^ k) for i in range(self.parts)])  17.6 us
    ppermute x15, starting transfers between devices, swap(): return lax.ppermute(value, AXES, [(i, i ^ k) for i in range(self.parts)])  14.4 us
    pallas_call x2, Pallas kernels, to_rows(): pl.pallas_call(body, grid=(samples,), in_specs=[per_sample()], out_specs=...  8.5 us
    unnamed x20, local copies, waits for them, and re-layouts  5.1 us
    pallas_call x2, Pallas kernels, to_columns(): pl.pallas_call(body, grid=(samples,), in_specs=[VMEM], out_specs=per_samp...  4.07 us
  transfers between devices with their start and end apart: 17, of which 10 were waited for; matrix products, arithmetic and copies ran while one was open for 0% of the time, Pallas kernels for 7%

profile of v1, /device:TPU:0, one launch (start us, length us, event | category | flops | bytes accessed | tf_op | source)
XLA Modules:
  0.0 192.8 jit_solution(15832053559515246730)
XLA Ops:
  0.6 3.0 %collective-permute-start.3 = (bf16[768,128]{1,0:T(8,128)(2,1)}, bf16[768,128]{1,0:T(8,128)(2,1)S(1)}, u32[]{:S(2)}, u32[]{:S(2)}) collective-permute-start(bf16[768,128]{1,0:T(8,128)(2,1)} %bitcast.7), channel_id=1, source_target_pairs={{0,1},{1,0},{2,3},{3,2},{4,5},{5,4},{6,7},{7,6},{8,9},{9,8},{10,11... | collective-permute-start | bytes 589832 | tf_op jit(solution)/shard_map/ppermute | solution.py:720
  3.7 3.0 %collective-permute-start.1 = (bf16[48,192]{1,0:T(8,128)(2,1)}, bf16[48,192]{1,0:T(8,128)(2,1)S(1)}, u32[]{:S(2)}, u32[]{:S(2)}) collective-permute-start(bf16[48,192]{1,0:T(8,128)(2,1)} %refs_0_), channel_id=1, source_target_pairs={{0,16},{1,17},{2,18},{3,19},{4,20},{5,21},{6,22},{7,23},{8,24},{9,... | collective-permute-start | bytes 55304 | tf_op jit(solution)/shard_map/ppermute | solution.py:564
  6.8 1.6 collective-permute-start
  8.3 1.4 copy-done.4
  9.7 2.0 %shard_map.109.refs_1_ = bf16[8,192,512]{2,1,0:T(8,128)(2,1)S(1)} custom-call(bf16[1904,384]{1,0:T(8,128)(2,1)S(1)} %copy-done.4), custom_call_target="tpu_custom_call" | custom-call | tf_op jit(solution)/shard_map/pallas_call | solution.py:489
  11.8 1.1 copy-done.1
  12.9 1.3 collective-permute-done.2.refs_3_
  14.2 2.5 %collective-permute-start.7 = (bf16[4,48,192]{2,1,0:T(8,128)(2,1)S(1)}, bf16[4,48,192]{2,1,0:T(8,128)(2,1)S(1)}, u32[]{:S(2)}, u32[]{:S(2)}) collective-permute-start(bf16[4,48,192]{2,1,0:T(8,128)(2,1)S(1)} %shard_map.110.refs_0_), channel_id=1, source_target_pairs={{0,5},{1,4},{2,7},{3,6},{4,1},{5,0},{6,3},{7,2},{8,13},{9,12},{10,... | collective-permute-start | bytes 221192 | tf_op jit(solution)/shard_map/ppermute | solution.py:564
  17.8 2.0 %shard_map.111.refs_2_ = bf16[8,192,512]{2,1,0:T(8,128)(2,1)S(1)} custom-call(bf16[1904,384]{1,0:T(8,128)(2,1)S(1)} %copy-done.5), custom_call_target="tpu_custom_call" | custom-call | tf_op jit(solution)/shard_map/pallas_call | solution.py:489
  19.8 1.2 copy-done.3
  22.0 1.7 collective-permute-done.8.refs_9_
  23.7 136.8 %shard_map.113 = (bf16[8,192,512]{2,1,0:T(8,128)(2,1)}, f32[8,192,512]{2,1,0:T(8,128)}, bf16[4,304,256]{2,1,0:T(8,128)(2,1)S(1)}, bf16[4,304,256]{2,1,0:T(8,128)(2,1)}) custom-call(s32[1]{0:T(128)} %bitcast.me_ref.refs_0_, bf16[8,192,512]{2,1,0:T(8,128)(2,1)} %copy-done.1, bf16[8,192,512]{2,1,0:T(8,128)(2,1)} %copy-done.3, f32[3,2,192]{2,1,0:T(2,128)S(1)} %copy-done.9, ...), custom_call_target="tpu_custom_call" | custom-call | flops 40000000000 | bytes 20000000 | tf_op jit(solution)/shard_map/pallas_call | solution.py:527
  160.7 2.1 %collective-permute-done.9.theirs = bf16[4,304,256]{2,1,0:T(8,128)(2,1)S(1)} collective-permute-done((bf16[4,304,256]{2,1,0:T(8,128)(2,1)}, bf16[4,304,256]{2,1,0:T(8,128)(2,1)S(1)}, u32[]{:S(2)}, u32[]{:S(2)}) %collective-permute-start.9) | collective-permute-done | bytes 622624 | tf_op jit(solution)/shard_map/ppermute | solution.py:564
  163.7 1.5 collective-permute-start.11
  165.2 1.3 collective-permute-start.12
  166.6 1.4 copy-done.2
  168.0 4.0 %shard_map.115 = bf16[1904,384]{1,0:T(8,128)(2,1)} custom-call(bf16[8,192,512]{2,1,0:T(8,128)(2,1)S(1)} %copy-done.2), custom_call_target="tpu_custom_call" | custom-call | tf_op jit(solution)/shard_map/pallas_call | solution.py:505
  172.0 1.4 collective-permute-done.12.refs_3_
  173.7 5.0 %collective-permute-done.13.theirs = bf16[272,256]{1,0:T(8,128)(2,1)S(1)} collective-permute-done((bf16[272,256]{1,0:T(8,128)(2,1)S(1)}, bf16[272,256]{1,0:T(8,128)(2,1)S(1)}, u32[]{:S(2)}, u32[]{:S(2)}) %collective-permute-start.13) | collective-permute-done | bytes 139296 | tf_op jit(solution)/shard_map/ppermute | solution.py:564
  178.7 1.3 collective-permute-start.14
  180.1 4.5 %shard_map.118 = f32[1904,384]{1,0:T(8,128)} custom-call(f32[8,192,512]{2,1,0:T(8,128)S(1)} %copy-done), custom_call_target="tpu_custom_call" | custom-call | tf_op jit(solution)/shard_map/pallas_call | solution.py:505
  184.5 0.9 collective-permute-done.14.theirs
  186.1 0.9 collective-permute-start.15
  187.0 3.5 %collective-permute-done.15.refs_1_ = bf16[1,160,256]{2,1,0:T(8,128)(2,1)S(1)} collective-permute-done((bf16[1,160,256]{2,1,0:T(8,128)(2,1)S(1)}, bf16[1,160,256]{2,1,0:T(8,128)(2,1)S(1)}, u32[]{:S(2)}, u32[]{:S(2)}) %collective-permute-start.15) | collective-permute-done | bytes 81952 | tf_op jit(solution)/shard_map/ppermute | solution.py:564
  (44 shorter events, 6.4 us)
Async XLA Ops:
  0.6 13.5 %collective-permute-start.3 = (bf16[768,128]{1,0:T(8,128)(2,1)}, bf16[768,128]{1,0:T(8,128)(2,1)S(1)}, u32[]{:S(2)}, u32[]{:S(2)}) collective-permute-start(bf16[768,128]{1,0:T(8,128)(2,1)} %bitcast.7), channel_id=1, source_target_pairs={{0,1},{1,0},{2,3},{3,2},{4,5},{5,4},{6,7},{7,6},{8,9},{9,8},{10,11... | collective-permute-start | bytes 589832 | tf_op jit(solution)/shard_map/ppermute | solution.py:720
  3.6 10.5 %collective-permute-start.4 = (bf16[2,192,128]{2,1,0:T(8,128)(2,1)}, bf16[2,192,128]{2,1,0:T(8,128)(2,1)S(1)}, u32[]{:S(2)}, u32[]{:S(2)}) collective-permute-start(bf16[2,192,128]{2,1,0:T(8,128)(2,1)} %bitcast.9), channel_id=1, source_target_pairs={{0,1},{1,0},{2,3},{3,2},{4,5},{5,4},{6,7},{7,6},{8,9},{9,8},{10,11... | collective-permute-start | bytes 294920 | tf_op jit(solution)/shard_map/ppermute | solution.py:721
  3.7 9.2 %collective-permute-start.1 = (bf16[48,192]{1,0:T(8,128)(2,1)}, bf16[48,192]{1,0:T(8,128)(2,1)S(1)}, u32[]{:S(2)}, u32[]{:S(2)}) collective-permute-start(bf16[48,192]{1,0:T(8,128)(2,1)} %refs_0_), channel_id=1, source_target_pairs={{0,16},{1,17},{2,18},{3,19},{4,20},{5,21},{6,22},{7,23},{8,24},{9,... | collective-permute-start | bytes 55304 | tf_op jit(solution)/shard_map/ppermute | solution.py:564
  6.8 6.2 %collective-permute-start = (bf16[48,192]{1,0:T(8,128)(2,1)}, bf16[48,192]{1,0:T(8,128)(2,1)S(1)}, u32[]{:S(2)}, u32[]{:S(2)}) collective-permute-start(bf16[48,192]{1,0:T(8,128)(2,1)} %refs_0_), channel_id=1, source_target_pairs={{0,8},{1,9},{2,10},{3,11},{4,12},{5,13},{6,14},{7,15},{8,0},{9,1},... | collective-permute-start | bytes 55304 | tf_op jit(solution)/shard_map/ppermute | solution.py:564
  8.3 5.8 %collective-permute-start.2 = (bf16[48,192]{1,0:T(8,128)(2,1)}, bf16[48,192]{1,0:T(8,128)(2,1)S(1)}, u32[]{:S(2)}, u32[]{:S(2)}) collective-permute-start(bf16[48,192]{1,0:T(8,128)(2,1)} %refs_0_), channel_id=1, source_target_pairs={{0,24},{1,25},{2,26},{3,27},{4,28},{5,29},{6,30},{7,31},{8,16},{9,... | collective-permute-start | bytes 55304 | tf_op jit(solution)/shard_map/ppermute | solution.py:564
  9.7 4.5 %copy-start.6 = (bf16[48,192]{1,0:T(8,128)(2,1)S(1)}, bf16[48,192]{1,0:T(8,128)(2,1)}, u32[]{:S(2)}) copy-start(bf16[48,192]{1,0:T(8,128)(2,1)} %refs_0_) | copy-start | bytes 55300
  9.7 8.1 %copy-start.5 = (bf16[1904,384]{1,0:T(8,128)(2,1)S(1)}, bf16[1904,384]{1,0:T(8,128)(2,1)}, u32[]{:S(2)}) copy-start(bf16[1904,384]{1,0:T(8,128)(2,1)} %rows_ref.3) | copy-start | bytes 4386820
  14.2 9.5 %copy-start.7 = (bf16[2,192,2,128]{3,2,1,0:T(2,128)(2,1)S(1)}, bf16[2,192,2,128]{3,2,1,0:T(2,128)(2,1)}, u32[]{:S(2)}) copy-start(bf16[2,192,2,128]{3,2,1,0:T(2,128)(2,1)} %param.9) | copy-start | bytes 589828
  14.2 9.5 %copy-start.8 = (bf16[2,128,192]{1,2,0:T(8,128)(2,1)S(1)}, bf16[2,128,192]{1,2,0:T(8,128)(2,1)}, u32[]{:S(2)}) copy-start(bf16[2,128,192]{1,2,0:T(8,128)(2,1)} %param.10) | copy-start | bytes 294916
  14.2 9.5 %copy-start.9 = (f32[3,2,192]{2,1,0:T(2,128)S(1)}, f32[3,2,192]{2,1,0:T(2,128)}, u32[]{:S(2)}) copy-start(f32[3,2,192]{2,1,0:T(2,128)} %refs_3_.1) | copy-start | bytes 13828
  14.2 6.8 %collective-permute-start.7 = (bf16[4,48,192]{2,1,0:T(8,128)(2,1)S(1)}, bf16[4,48,192]{2,1,0:T(8,128)(2,1)S(1)}, u32[]{:S(2)}, u32[]{:S(2)}) collective-permute-start(bf16[4,48,192]{2,1,0:T(8,128)(2,1)S(1)} %shard_map.110.refs_0_), channel_id=1, source_target_pairs={{0,5},{1,4},{2,7},{3,6},{4,1},{5,0},{6,3},{7,2},{8,13},{9,12},{10,... | collective-permute-start | bytes 221192 | tf_op jit(solution)/shard_map/ppermute | solution.py:564
  16.8 4.6 %collective-permute-start.6 = (bf16[4,48,192]{2,1,0:T(8,128)(2,1)S(1)}, bf16[4,48,192]{2,1,0:T(8,128)(2,1)S(1)}, u32[]{:S(2)}, u32[]{:S(2)}) collective-permute-start(bf16[4,48,192]{2,1,0:T(8,128)(2,1)S(1)} %shard_map.110.refs_0_), channel_id=1, source_target_pairs={{0,4},{1,5},{2,6},{3,7},{4,0},{5,1},{6,2},{7,3},{8,12},{9,13},{10,... | collective-permute-start | bytes 221192 | tf_op jit(solution)/shard_map/ppermute | solution.py:564
  17.3 4.6 %collective-permute-start.5 = (bf16[4,48,192]{2,1,0:T(8,128)(2,1)S(1)}, bf16[4,48,192]{2,1,0:T(8,128)(2,1)S(1)}, u32[]{:S(2)}, u32[]{:S(2)}) collective-permute-start(bf16[4,48,192]{2,1,0:T(8,128)(2,1)S(1)} %shard_map.110.refs_0_), channel_id=1, source_target_pairs={{0,1},{1,0},{2,3},{3,2},{4,5},{5,4},{6,7},{7,6},{8,9},{9,8},{10,11... | collective-permute-start | bytes 221192 | tf_op jit(solution)/shard_map/ppermute | solution.py:564
  21.9 1.8 collective-permute-start.8
  160.5 2.3 %collective-permute-start.9 = (bf16[4,304,256]{2,1,0:T(8,128)(2,1)}, bf16[4,304,256]{2,1,0:T(8,128)(2,1)S(1)}, u32[]{:S(2)}, u32[]{:S(2)}) collective-permute-start(bf16[4,304,256]{2,1,0:T(8,128)(2,1)} %get-tuple-element.55), channel_id=1, source_target_pairs={{0,2},{1,3},{2,0},{3,1},{4,6},{5,7},{6,4},{7,5},{8,10},{9,11},{10,... | collective-permute-start | bytes 1867784 | tf_op jit(solution)/shard_map/ppermute | solution.py:564
  163.0 9.0 %collective-permute-start.10 = (bf16[304,256]{1,0:T(8,128)(2,1)S(1)}, bf16[304,256]{1,0:T(8,128)(2,1)S(1)}, u32[]{:S(2)}, u32[]{:S(2)}) collective-permute-start(bf16[304,256]{1,0:T(8,128)(2,1)S(1)} %get-tuple-element.57), channel_id=1, source_target_pairs={{0,1},{1,0},{2,3},{3,2},{4,5},{5,4},{6,7},{7,6},{8,9},{9,8},{10,11... | collective-permute-start | bytes 466952 | tf_op jit(solution)/shard_map/ppermute | solution.py:564
  163.7 8.3 %collective-permute-start.11 = (bf16[304,256]{1,0:T(8,128)(2,1)S(1)}, bf16[304,256]{1,0:T(8,128)(2,1)S(1)}, u32[]{:S(2)}, u32[]{:S(2)}) collective-permute-start(bf16[304,256]{1,0:T(8,128)(2,1)S(1)} %get-tuple-element.58), channel_id=1, source_target_pairs={{0,4},{1,5},{2,6},{3,7},{4,0},{5,1},{6,2},{7,3},{8,12},{9,13},{10,... | collective-permute-start | bytes 466952 | tf_op jit(solution)/shard_map/ppermute | solution.py:564
  165.2 8.2 %collective-permute-start.12 = (bf16[304,256]{1,0:T(8,128)(2,1)S(1)}, bf16[304,256]{1,0:T(8,128)(2,1)S(1)}, u32[]{:S(2)}, u32[]{:S(2)}) collective-permute-start(bf16[304,256]{1,0:T(8,128)(2,1)S(1)} %get-tuple-element.59), channel_id=1, source_target_pairs={{0,5},{1,4},{2,7},{3,6},{4,1},{5,0},{6,3},{7,2},{8,13},{9,12},{10,... | collective-permute-start | bytes 466952 | tf_op jit(solution)/shard_map/ppermute | solution.py:564
  166.5 1.4 copy-start.2
  168.0 12.1 %copy-start = (f32[8,192,512]{2,1,0:T(8,128)S(1)}, f32[8,192,512]{2,1,0:T(8,128)}, u32[]{:S(2)}) copy-start(f32[8,192,512]{2,1,0:T(8,128)} %get-tuple-element.69.columns_ref) | copy-start | bytes 9437188
  173.6 5.1 %collective-permute-start.13 = (bf16[272,256]{1,0:T(8,128)(2,1)S(1)}, bf16[272,256]{1,0:T(8,128)(2,1)S(1)}, u32[]{:S(2)}, u32[]{:S(2)}) collective-permute-start(bf16[272,256]{1,0:T(8,128)(2,1)S(1)} %get-tuple-element.67), channel_id=1, source_target_pairs={{0,8},{1,9},{2,10},{3,11},{4,12},{5,13},{6,14},{7,15},{8,0},{9,1},... | collective-permute-start | bytes 417800 | tf_op jit(solution)/shard_map/ppermute | solution.py:564
  178.7 6.7 %collective-permute-start.14 = (bf16[224,256]{1,0:T(8,128)(2,1)S(1)}, bf16[224,256]{1,0:T(8,128)(2,1)S(1)}, u32[]{:S(2)}, u32[]{:S(2)}) collective-permute-start(bf16[224,256]{1,0:T(8,128)(2,1)S(1)} %get-tuple-element.68), channel_id=1, source_target_pairs={{0,16},{1,17},{2,18},{3,19},{4,20},{5,21},{6,22},{7,23},{8,24},{9,... | collective-permute-start | bytes 344072 | tf_op jit(solution)/shard_map/ppermute | solution.py:564
  186.1 4.4 %collective-permute-start.15 = (bf16[1,160,256]{2,1,0:T(8,128)(2,1)S(1)}, bf16[1,160,256]{2,1,0:T(8,128)(2,1)S(1)}, u32[]{:S(2)}, u32[]{:S(2)}) collective-permute-start(bf16[1,160,256]{2,1,0:T(8,128)(2,1)S(1)} %get-tuple-element.75.refs_0_), channel_id=1, source_target_pairs={{0,4},{1,5},{2,6},{3,7},{4,0},{5,1},{6,2},{7,3},{8,12},{9,13},{10,... | collective-permute-start | bytes 245768 | tf_op jit(solution)/shard_map/ppermute | solution.py:564
  190.5 1.5 collective-permute-start.16
  (3 other events, 3.7 us)

commit v2 on v1

--- a/solution.py
+++ b/solution.py
@@ -325,7 +325,7 @@
     *WORK,
     ((HEADS, 2 * KEYS, SLOT), bf16),
     ((WIDE, LANES), bf16),
-    ((LAYERS, 2 * FF, LANES), f32),
+    ((LAYERS, 2 * FF, LANES), bf16),
     ((2 * LAYERS * D, FFH), f32),
 ]
 
@@ -413,7 +413,7 @@
         normed, unit_f, inv_f = norm_forward(stream, gain_of(2 * layer), shift_of(2 * layer))
         ffn_b = normed.astype(bf16)
         mixed = mm(win_t[layer], ffn_b)
-        mixed_ref[layer] = mixed
+        mixed_ref[layer] = mixed.astype(bf16)
         hidden = []
         for p in range(2):
             value = mixed[FF * p : FF * p + FFH]
@@ -432,8 +432,8 @@
         d_hidden = mm(wout[layer], grad_b)
         d_mixed = []
         for p in range(2):
-            value = mixed_ref[layer, FF * p : FF * p + FFH]
-            gate = mixed_ref[layer, FF * p + FFH : FF * (p + 1)]
+            value = mixed_ref[layer, FF * p : FF * p + FFH].astype(f32)
+            gate = mixed_ref[layer, FF * p + FFH : FF * (p + 1)].astype(f32)
             part = d_hidden[FFH * p : FFH * (p + 1)]
             sig = sigmoid(gate)
             d_mixed.append((part * (gate * sig)).astype(bf16))

time: 193 us -> 194 us (level)
  transfers between devices with their start and end apart: 17 -> 17, of which waited for: 10 -> 10; matrix products, arithmetic and copies ran while one was open for 0% -> 0% of each run, Pallas kernels for 7% -> 6%
where the time goes in v2:
time: 194 us
  Pallas kernels  152 us (78%)
  waiting for transfers between devices  17.6 us (9%)
  starting transfers between devices  17.4 us (9%)
  local copies, waits for them, and re-layouts  5.7 us (3%)
    pallas_call x1, Pallas kernels, run_main(): pl.pallas_call(body, grid=(samples,), in_specs=[SMEM, per_sample(), per_s...  138 us
    ppermute x15, waiting for transfers between devices, swap(): return lax.ppermute(value, AXES, [(i, i ^ k) for i in range(self.parts)])  17.6 us
    ppermute x15, starting transfers between devices, swap(): return lax.ppermute(value, AXES, [(i, i ^ k) for i in range(self.parts)])  14.4 us
    pallas_call x2, Pallas kernels, to_rows(): pl.pallas_call(body, grid=(samples,), in_specs=[per_sample()], out_specs=...  8.5 us
    unnamed x20, local copies, waits for them, and re-layouts  5.1 us
    pallas_call x2, Pallas kernels, to_columns(): pl.pallas_call(body, grid=(samples,), in_specs=[VMEM], out_specs=per_samp...  4.07 us
  transfers between devices with their start and end apart: 17, of which 10 were waited for; matrix products, arithmetic and copies ran while one was open for 0% of the time, Pallas kernels for 6%

profile of v2, /device:TPU:0, one launch (start us, length us, event | category | flops | bytes accessed | tf_op | source)
XLA Modules:
  0.0 193.6 jit_solution(2471565961976798206)
XLA Ops:
  0.6 3.0 %collective-permute-start.3 = (bf16[768,128]{1,0:T(8,128)(2,1)}, bf16[768,128]{1,0:T(8,128)(2,1)S(1)}, u32[]{:S(2)}, u32[]{:S(2)}) collective-permute-start(bf16[768,128]{1,0:T(8,128)(2,1)} %bitcast.7), channel_id=1, source_target_pairs={{0,1},{1,0},{2,3},{3,2},{4,5},{5,4},{6,7},{7,6},{8,9},{9,8},{10,11... | collective-permute-start | bytes 589832 | tf_op jit(solution)/shard_map/ppermute | solution.py:720
  3.7 3.0 %collective-permute-start.1 = (bf16[48,192]{1,0:T(8,128)(2,1)}, bf16[48,192]{1,0:T(8,128)(2,1)S(1)}, u32[]{:S(2)}, u32[]{:S(2)}) collective-permute-start(bf16[48,192]{1,0:T(8,128)(2,1)} %refs_0_), channel_id=1, source_target_pairs={{0,16},{1,17},{2,18},{3,19},{4,20},{5,21},{6,22},{7,23},{8,24},{9,... | collective-permute-start | bytes 55304 | tf_op jit(solution)/shard_map/ppermute | solution.py:564
  6.8 1.6 collective-permute-start
  8.3 1.4 copy-done.4
  9.7 2.0 %shard_map.109.refs_1_ = bf16[8,192,512]{2,1,0:T(8,128)(2,1)S(1)} custom-call(bf16[1904,384]{1,0:T(8,128)(2,1)S(1)} %copy-done.4), custom_call_target="tpu_custom_call" | custom-call | tf_op jit(solution)/shard_map/pallas_call | solution.py:489
  11.8 1.1 copy-done.1
  12.9 1.3 collective-permute-done.2.refs_3_
  14.2 2.5 %collective-permute-start.7 = (bf16[4,48,192]{2,1,0:T(8,128)(2,1)S(1)}, bf16[4,48,192]{2,1,0:T(8,128)(2,1)S(1)}, u32[]{:S(2)}, u32[]{:S(2)}) collective-permute-start(bf16[4,48,192]{2,1,0:T(8,128)(2,1)S(1)} %shard_map.110.refs_0_), channel_id=1, source_target_pairs={{0,5},{1,4},{2,7},{3,6},{4,1},{5,0},{6,3},{7,2},{8,13},{9,12},{10,... | collective-permute-start | bytes 221192 | tf_op jit(solution)/shard_map/ppermute | solution.py:564
  17.8 2.0 %shard_map.111.refs_2_ = bf16[8,192,512]{2,1,0:T(8,128)(2,1)S(1)} custom-call(bf16[1904,384]{1,0:T(8,128)(2,1)S(1)} %copy-done.5), custom_call_target="tpu_custom_call" | custom-call | tf_op jit(solution)/shard_map/pallas_call | solution.py:489
  19.8 1.2 copy-done.3
  22.0 1.7 collective-permute-done.8.refs_9_
  23.7 137.6 %shard_map.113 = (bf16[8,192,512]{2,1,0:T(8,128)(2,1)}, f32[8,192,512]{2,1,0:T(8,128)}, bf16[4,304,256]{2,1,0:T(8,128)(2,1)S(1)}, bf16[4,304,256]{2,1,0:T(8,128)(2,1)}) custom-call(s32[1]{0:T(128)} %bitcast.me_ref.refs_0_, bf16[8,192,512]{2,1,0:T(8,128)(2,1)} %copy-done.1, bf16[8,192,512]{2,1,0:T(8,128)(2,1)} %copy-done.3, f32[3,2,192]{2,1,0:T(2,128)S(1)} %copy-done.9, ...), custom_call_target="tpu_custom_call" | custom-call | flops 40000000000 | bytes 20000000 | tf_op jit(solution)/shard_map/pallas_call | solution.py:527
  161.4 2.1 %collective-permute-done.9.theirs = bf16[4,304,256]{2,1,0:T(8,128)(2,1)S(1)} collective-permute-done((bf16[4,304,256]{2,1,0:T(8,128)(2,1)}, bf16[4,304,256]{2,1,0:T(8,128)(2,1)S(1)}, u32[]{:S(2)}, u32[]{:S(2)}) %collective-permute-start.9) | collective-permute-done | bytes 622624 | tf_op jit(solution)/shard_map/ppermute | solution.py:564
  164.4 1.5 collective-permute-start.11
  166.0 1.3 collective-permute-start.12
  167.3 1.4 copy-done.2
  168.7 4.0 %shard_map.115 = bf16[1904,384]{1,0:T(8,128)(2,1)} custom-call(bf16[8,192,512]{2,1,0:T(8,128)(2,1)S(1)} %copy-done.2), custom_call_target="tpu_custom_call" | custom-call | tf_op jit(solution)/shard_map/pallas_call | solution.py:505
  172.8 1.4 collective-permute-done.12.refs_3_
  174.4 5.0 %collective-permute-done.13.theirs = bf16[272,256]{1,0:T(8,128)(2,1)S(1)} collective-permute-done((bf16[272,256]{1,0:T(8,128)(2,1)S(1)}, bf16[272,256]{1,0:T(8,128)(2,1)S(1)}, u32[]{:S(2)}, u32[]{:S(2)}) %collective-permute-start.13) | collective-permute-done | bytes 139296 | tf_op jit(solution)/shard_map/ppermute | solution.py:564
  179.5 1.3 collective-permute-start.14
  180.8 4.5 %shard_map.118 = f32[1904,384]{1,0:T(8,128)} custom-call(f32[8,192,512]{2,1,0:T(8,128)S(1)} %copy-done), custom_call_target="tpu_custom_call" | custom-call | tf_op jit(solution)/shard_map/pallas_call | solution.py:505
  185.3 0.9 collective-permute-done.14.theirs
  186.8 0.9 collective-permute-start.15
  187.7 3.5 %collective-permute-done.15.refs_1_ = bf16[1,160,256]{2,1,0:T(8,128)(2,1)S(1)} collective-permute-done((bf16[1,160,256]{2,1,0:T(8,128)(2,1)S(1)}, bf16[1,160,256]{2,1,0:T(8,128)(2,1)S(1)}, u32[]{:S(2)}, u32[]{:S(2)}) %collective-permute-start.15) | collective-permute-done | bytes 81952 | tf_op jit(solution)/shard_map/ppermute | solution.py:564
  (44 shorter events, 6.4 us)
Async XLA Ops:
  0.6 13.5 %collective-permute-start.3 = (bf16[768,128]{1,0:T(8,128)(2,1)}, bf16[768,128]{1,0:T(8,128)(2,1)S(1)}, u32[]{:S(2)}, u32[]{:S(2)}) collective-permute-start(bf16[768,128]{1,0:T(8,128)(2,1)} %bitcast.7), channel_id=1, source_target_pairs={{0,1},{1,0},{2,3},{3,2},{4,5},{5,4},{6,7},{7,6},{8,9},{9,8},{10,11... | collective-permute-start | bytes 589832 | tf_op jit(solution)/shard_map/ppermute | solution.py:720
  3.6 10.5 %collective-permute-start.4 = (bf16[2,192,128]{2,1,0:T(8,128)(2,1)}, bf16[2,192,128]{2,1,0:T(8,128)(2,1)S(1)}, u32[]{:S(2)}, u32[]{:S(2)}) collective-permute-start(bf16[2,192,128]{2,1,0:T(8,128)(2,1)} %bitcast.9), channel_id=1, source_target_pairs={{0,1},{1,0},{2,3},{3,2},{4,5},{5,4},{6,7},{7,6},{8,9},{9,8},{10,11... | collective-permute-start | bytes 294920 | tf_op jit(solution)/shard_map/ppermute | solution.py:721
  3.7 9.2 %collective-permute-start.1 = (bf16[48,192]{1,0:T(8,128)(2,1)}, bf16[48,192]{1,0:T(8,128)(2,1)S(1)}, u32[]{:S(2)}, u32[]{:S(2)}) collective-permute-start(bf16[48,192]{1,0:T(8,128)(2,1)} %refs_0_), channel_id=1, source_target_pairs={{0,16},{1,17},{2,18},{3,19},{4,20},{5,21},{6,22},{7,23},{8,24},{9,... | collective-permute-start | bytes 55304 | tf_op jit(solution)/shard_map/ppermute | solution.py:564
  6.8 6.2 %collective-permute-start = (bf16[48,192]{1,0:T(8,128)(2,1)}, bf16[48,192]{1,0:T(8,128)(2,1)S(1)}, u32[]{:S(2)}, u32[]{:S(2)}) collective-permute-start(bf16[48,192]{1,0:T(8,128)(2,1)} %refs_0_), channel_id=1, source_target_pairs={{0,8},{1,9},{2,10},{3,11},{4,12},{5,13},{6,14},{7,15},{8,0},{9,1},... | collective-permute-start | bytes 55304 | tf_op jit(solution)/shard_map/ppermute | solution.py:564
  8.3 5.8 %collective-permute-start.2 = (bf16[48,192]{1,0:T(8,128)(2,1)}, bf16[48,192]{1,0:T(8,128)(2,1)S(1)}, u32[]{:S(2)}, u32[]{:S(2)}) collective-permute-start(bf16[48,192]{1,0:T(8,128)(2,1)} %refs_0_), channel_id=1, source_target_pairs={{0,24},{1,25},{2,26},{3,27},{4,28},{5,29},{6,30},{7,31},{8,16},{9,... | collective-permute-start | bytes 55304 | tf_op jit(solution)/shard_map/ppermute | solution.py:564
  9.7 4.5 %copy-start.6 = (bf16[48,192]{1,0:T(8,128)(2,1)S(1)}, bf16[48,192]{1,0:T(8,128)(2,1)}, u32[]{:S(2)}) copy-start(bf16[48,192]{1,0:T(8,128)(2,1)} %refs_0_) | copy-start | bytes 55300
  9.7 8.1 %copy-start.5 = (bf16[1904,384]{1,0:T(8,128)(2,1)S(1)}, bf16[1904,384]{1,0:T(8,128)(2,1)}, u32[]{:S(2)}) copy-start(bf16[1904,384]{1,0:T(8,128)(2,1)} %rows_ref.3) | copy-start | bytes 4386820
  14.2 9.5 %copy-start.7 = (bf16[2,192,2,128]{3,2,1,0:T(2,128)(2,1)S(1)}, bf16[2,192,2,128]{3,2,1,0:T(2,128)(2,1)}, u32[]{:S(2)}) copy-start(bf16[2,192,2,128]{3,2,1,0:T(2,128)(2,1)} %param.9) | copy-start | bytes 589828
  14.2 9.5 %copy-start.8 = (bf16[2,128,192]{1,2,0:T(8,128)(2,1)S(1)}, bf16[2,128,192]{1,2,0:T(8,128)(2,1)}, u32[]{:S(2)}) copy-start(bf16[2,128,192]{1,2,0:T(8,128)(2,1)} %param.10) | copy-start | bytes 294916
  14.2 9.5 %copy-start.9 = (f32[3,2,192]{2,1,0:T(2,128)S(1)}, f32[3,2,192]{2,1,0:T(2,128)}, u32[]{:S(2)}) copy-start(f32[3,2,192]{2,1,0:T(2,128)} %refs_3_.1) | copy-start | bytes 13828
  14.2 6.8 %collective-permute-start.7 = (bf16[4,48,192]{2,1,0:T(8,128)(2,1)S(1)}, bf16[4,48,192]{2,1,0:T(8,128)(2,1)S(1)}, u32[]{:S(2)}, u32[]{:S(2)}) collective-permute-start(bf16[4,48,192]{2,1,0:T(8,128)(2,1)S(1)} %shard_map.110.refs_0_), channel_id=1, source_target_pairs={{0,5},{1,4},{2,7},{3,6},{4,1},{5,0},{6,3},{7,2},{8,13},{9,12},{10,... | collective-permute-start | bytes 221192 | tf_op jit(solution)/shard_map/ppermute | solution.py:564
  16.8 4.6 %collective-permute-start.6 = (bf16[4,48,192]{2,1,0:T(8,128)(2,1)S(1)}, bf16[4,48,192]{2,1,0:T(8,128)(2,1)S(1)}, u32[]{:S(2)}, u32[]{:S(2)}) collective-permute-start(bf16[4,48,192]{2,1,0:T(8,128)(2,1)S(1)} %shard_map.110.refs_0_), channel_id=1, source_target_pairs={{0,4},{1,5},{2,6},{3,7},{4,0},{5,1},{6,2},{7,3},{8,12},{9,13},{10,... | collective-permute-start | bytes 221192 | tf_op jit(solution)/shard_map/ppermute | solution.py:564
  17.3 4.6 %collective-permute-start.5 = (bf16[4,48,192]{2,1,0:T(8,128)(2,1)S(1)}, bf16[4,48,192]{2,1,0:T(8,128)(2,1)S(1)}, u32[]{:S(2)}, u32[]{:S(2)}) collective-permute-start(bf16[4,48,192]{2,1,0:T(8,128)(2,1)S(1)} %shard_map.110.refs_0_), channel_id=1, source_target_pairs={{0,1},{1,0},{2,3},{3,2},{4,5},{5,4},{6,7},{7,6},{8,9},{9,8},{10,11... | collective-permute-start | bytes 221192 | tf_op jit(solution)/shard_map/ppermute | solution.py:564
  21.9 1.8 collective-permute-start.8
  161.3 2.3 %collective-permute-start.9 = (bf16[4,304,256]{2,1,0:T(8,128)(2,1)}, bf16[4,304,256]{2,1,0:T(8,128)(2,1)S(1)}, u32[]{:S(2)}, u32[]{:S(2)}) collective-permute-start(bf16[4,304,256]{2,1,0:T(8,128)(2,1)} %get-tuple-element.55), channel_id=1, source_target_pairs={{0,2},{1,3},{2,0},{3,1},{4,6},{5,7},{6,4},{7,5},{8,10},{9,11},{10,... | collective-permute-start | bytes 1867784 | tf_op jit(solution)/shard_map/ppermute | solution.py:564
  163.7 9.0 %collective-permute-start.10 = (bf16[304,256]{1,0:T(8,128)(2,1)S(1)}, bf16[304,256]{1,0:T(8,128)(2,1)S(1)}, u32[]{:S(2)}, u32[]{:S(2)}) collective-permute-start(bf16[304,256]{1,0:T(8,128)(2,1)S(1)} %get-tuple-element.57), channel_id=1, source_target_pairs={{0,1},{1,0},{2,3},{3,2},{4,5},{5,4},{6,7},{7,6},{8,9},{9,8},{10,11... | collective-permute-start | bytes 466952 | tf_op jit(solution)/shard_map/ppermute | solution.py:564
  164.4 8.3 %collective-permute-start.11 = (bf16[304,256]{1,0:T(8,128)(2,1)S(1)}, bf16[304,256]{1,0:T(8,128)(2,1)S(1)}, u32[]{:S(2)}, u32[]{:S(2)}) collective-permute-start(bf16[304,256]{1,0:T(8,128)(2,1)S(1)} %get-tuple-element.58), channel_id=1, source_target_pairs={{0,4},{1,5},{2,6},{3,7},{4,0},{5,1},{6,2},{7,3},{8,12},{9,13},{10,... | collective-permute-start | bytes 466952 | tf_op jit(solution)/shard_map/ppermute | solution.py:564
  166.0 8.2 %collective-permute-start.12 = (bf16[304,256]{1,0:T(8,128)(2,1)S(1)}, bf16[304,256]{1,0:T(8,128)(2,1)S(1)}, u32[]{:S(2)}, u32[]{:S(2)}) collective-permute-start(bf16[304,256]{1,0:T(8,128)(2,1)S(1)} %get-tuple-element.59), channel_id=1, source_target_pairs={{0,5},{1,4},{2,7},{3,6},{4,1},{5,0},{6,3},{7,2},{8,13},{9,12},{10,... | collective-permute-start | bytes 466952 | tf_op jit(solution)/shard_map/ppermute | solution.py:564
  167.3 1.4 copy-start.2
  168.7 12.1 %copy-start = (f32[8,192,512]{2,1,0:T(8,128)S(1)}, f32[8,192,512]{2,1,0:T(8,128)}, u32[]{:S(2)}) copy-start(f32[8,192,512]{2,1,0:T(8,128)} %get-tuple-element.69.columns_ref) | copy-start | bytes 9437188
  174.3 5.1 %collective-permute-start.13 = (bf16[272,256]{1,0:T(8,128)(2,1)S(1)}, bf16[272,256]{1,0:T(8,128)(2,1)S(1)}, u32[]{:S(2)}, u32[]{:S(2)}) collective-permute-start(bf16[272,256]{1,0:T(8,128)(2,1)S(1)} %get-tuple-element.67), channel_id=1, source_target_pairs={{0,8},{1,9},{2,10},{3,11},{4,12},{5,13},{6,14},{7,15},{8,0},{9,1},... | collective-permute-start | bytes 417800 | tf_op jit(solution)/shard_map/ppermute | solution.py:564
  179.5 6.7 %collective-permute-start.14 = (bf16[224,256]{1,0:T(8,128)(2,1)S(1)}, bf16[224,256]{1,0:T(8,128)(2,1)S(1)}, u32[]{:S(2)}, u32[]{:S(2)}) collective-permute-start(bf16[224,256]{1,0:T(8,128)(2,1)S(1)} %get-tuple-element.68), channel_id=1, source_target_pairs={{0,16},{1,17},{2,18},{3,19},{4,20},{5,21},{6,22},{7,23},{8,24},{9,... | collective-permute-start | bytes 344072 | tf_op jit(solution)/shard_map/ppermute | solution.py:564
  186.8 4.4 %collective-permute-start.15 = (bf16[1,160,256]{2,1,0:T(8,128)(2,1)S(1)}, bf16[1,160,256]{2,1,0:T(8,128)(2,1)S(1)}, u32[]{:S(2)}, u32[]{:S(2)}) collective-permute-start(bf16[1,160,256]{2,1,0:T(8,128)(2,1)S(1)} %get-tuple-element.75.refs_0_), channel_id=1, source_target_pairs={{0,4},{1,5},{2,6},{3,7},{4,0},{5,1},{6,2},{7,3},{8,12},{9,13},{10,... | collective-permute-start | bytes 245768 | tf_op jit(solution)/shard_map/ppermute | solution.py:564
  191.3 1.5 collective-permute-start.16
  (3 other events, 3.7 us)
